TPU v7x, 512 devices: a whole 4x8x8 slice. The times are simulated.
512 devices in a mesh: rows: 128 (over y, z_hi, x), cols: 4 (over z_lo, core).
Axes of the slice: x: 4, y: 8, z: 8 (z_hi: 4, z_lo: 2; z = z_hi * 2 + z_lo), core: 2. Of those that a mesh axis runs over, the one named last changes fastest.
Arguments:
- fine_noisy: bfloat16 [1024, 128, 256], P('rows', 'cols'), may hold values from -6 to 6
- fine_weight: bfloat16 [2304, 256], P(None, 'cols'), may hold values from -0.125 to 0.125
- projection: bfloat16 [512, 256], P(None, 'cols'), may hold values from -0.25 to 0.25
- mid_noisy: bfloat16 [256, 32, 512], P('rows', 'cols'), may hold values from -6 to 6
- teacher_weight: bfloat16 [4608, 512], P(None, 'cols'), may hold values from -0.09375 to 0.09375
- student_weight: bfloat16 [4608, 512], P(None, 'cols'), may hold values from -0.09375 to 0.09375
- steps: int32 [3], replicated, may hold values from 401 to 999, as said below
- cotangent: bfloat16 [1024, 128, 256], P('rows', 'cols'), may hold values from -6 to 6
Outputs:
- fine_out: bfloat16 [1024, 128, 256], P('rows', 'cols')
- grad_input: bfloat16 [1024, 128, 256], P('rows', 'cols')
- grad_weight: float32 [2304, 256], P('rows')
- gap: bfloat16 [256, 32, 512], P('rows', 'cols')
Inputs may be any that keep to these rules, and one draw needn't show every extreme that they name: steps[0] is 999; each later index lies 150 to 299 below the one before it.
All inputs are finite; a program needn't handle non-finite values.
Results may differ from a plain program's by a relative error of at most 0.012.
Values may be sent and summed in bfloat16 or wider, within the bound.
No kernel may reach another device: no remote copies, remote signals or barrier semaphores. Data moves between devices by JAX's collectives and lax.ppermute only.
A program may use at most 64 MiB of HBM per device.

v0:
```python
import math

import jax
import jax.numpy as jnp
from jax import lax
from jax.sharding import PartitionSpec as P


def extended(block, sides, width):
    for axis, dim in sides:
        count = lax.axis_size(axis)
        forward = [(i, i + 1) for i in range(count - 1)]
        backward = [(target, source) for source, target in forward]
        low = lax.ppermute(
            lax.slice_in_dim(block, block.shape[dim] - width, None, axis=dim), axis, forward
        )
        high = lax.ppermute(lax.slice_in_dim(block, 0, width, axis=dim), axis, backward)
        block = jnp.concatenate([low, block, high], axis=dim)
    return block


def embed(step_index, channels):
    half = channels // 2
    freqs = jnp.exp(-math.log(10000.0) * jnp.arange(half).astype(jnp.float32) / half)
    angles = step_index.astype(jnp.float32) * freqs
    return jnp.concatenate([jnp.sin(angles), jnp.cos(angles)])


def patches(padded, height, width):
    return jnp.concatenate(
        [
            padded[..., row_shift : row_shift + height, col_shift : col_shift + width, :]
            for row_shift in range(3)
            for col_shift in range(3)
        ],
        axis=-1,
    )


def mid_terms(field, weights):
    padded = extended(field, (("rows", 0), ("cols", 1)), 1)
    height, width = (field.shape[0], field.shape[1])
    stacked = jnp.stack(weights)
    tiles = patches(padded, height, width)
    return jnp.einsum(
        "ijk,wkc->wijc",
        tiles,
        lax.all_gather(stacked, "cols", axis=2, tiled=True),
        preferred_element_type=jnp.float32,
    )


def fine_padded(field):
    return extended(field, (("rows", 0), ("cols", 1)), 1)


def on_device(
    fine_noisy, fine_weight, projection, mid_noisy, teacher_weight, student_weight, steps, cotangent
):
    fine_rows, fine_cols, fine_ch = fine_noisy.shape
    mid_rows, mid_cols, channels = mid_noisy.shape
    full_weight, full_projection = (
        lax.all_gather(fine_weight, "cols", axis=1, tiled=True),
        lax.all_gather(projection, "cols", axis=1, tiled=True),
    )
    blocks = full_weight.reshape(9, fine_ch, fine_ch)[::-1]
    back_weight = jnp.transpose(blocks, (0, 2, 1)).reshape(9 * fine_ch, fine_ch)
    cot_patches = patches(fine_padded(cotangent), fine_rows, fine_cols).reshape(-1, 9 * fine_ch)
    grad_input = jnp.dot(cot_patches, back_weight, preferred_element_type=jnp.float32)
    grad_input = grad_input.reshape(fine_rows, fine_cols, fine_ch).astype(jnp.bfloat16)
    times = steps.astype(jnp.float32)
    delta_one = (times[1] - times[0]) / 1000.0
    delta_two = (times[2] - times[1]) / 1000.0
    anchor = mid_noisy.astype(jnp.float32)
    first_in = jax.nn.silu(anchor + embed(steps[0], channels)).astype(jnp.bfloat16)
    first = mid_terms(first_in, (teacher_weight, student_weight))
    middle = anchor + delta_one * first[0]
    second_in = jax.nn.silu(middle + embed(steps[1], channels)).astype(jnp.bfloat16)
    second = mid_terms(second_in, (teacher_weight,))
    target = middle + delta_two * second[0]
    gap = (target - (anchor + (delta_one + delta_two) * first[1])).astype(jnp.bfloat16)
    lifted = jnp.dot(
        target.astype(jnp.bfloat16).reshape(-1, channels),
        full_projection,
        preferred_element_type=jnp.float32,
    )
    lifted = lifted.reshape(mid_rows, mid_cols, fine_ch)
    lifted = jnp.repeat(jnp.repeat(lifted, 4, axis=0), 4, axis=1)
    fine_in = (fine_noisy.astype(jnp.float32) + lifted).astype(jnp.bfloat16)
    in_patches = patches(fine_padded(fine_in), fine_rows, fine_cols).reshape(-1, 9 * fine_ch)
    fine_out = jnp.dot(in_patches, full_weight, preferred_element_type=jnp.float32)
    fine_out = fine_out.reshape(fine_rows, fine_cols, fine_ch).astype(jnp.bfloat16)
    cot_flat = cotangent.reshape(-1, fine_ch)
    scale = 1.0 / math.sqrt(fine_rows * fine_cols * lax.axis_size("rows") * lax.axis_size("cols"))
    share = lax.psum_scatter(
        jnp.dot(in_patches.T, cot_flat, preferred_element_type=jnp.float32) * scale,
        "rows",
        scatter_dimension=0,
        tiled=True,
    )
    grad_weight = lax.psum(share, "cols")
    return (fine_out, grad_input, grad_weight, gap)


def solution(mesh):
    placed = (
        P("rows", "cols", None),
        P(None, "cols"),
        P(None, "cols"),
        P("rows", "cols", None),
        P(None, "cols"),
        P(None, "cols"),
        P(),
        P("rows", "cols", None),
    )
    return jax.shard_map(
        on_device,
        mesh=mesh,
        in_specs=placed,
        out_specs=(
            P("rows", "cols", None),
            P("rows", "cols", None),
            P("rows", None),
            P("rows", "cols", None),
        ),
        check_vma=False,
    )
```

profile of v0, /device:TPU:1, one launch (start us, length us, event | category | flops | bytes accessed | tf_op | source)
XLA Modules:
  0.0 771.0 jit_solution(12891796551188240080)
XLA Ops:
  7.2 3.2 pad_maximum_fusion
  12.7 3.9 collective-permute-start
  16.6 1.3 collective-permute-start.1
  17.9 21.9 %collective-permute-start.12 = (bf16[1,32,256]{2,1,0:T(8,128)(2,1)S(1)}, bf16[1,32,256]{2,1,0:T(8,128)(2,1)S(1)}, u32[]{:S(2)}, u32[]{:S(2)}) collective-permute-start(bf16[1,32,256]{2,1,0:T(8,128)(2,1)S(1)} %get-tuple-element.11), channel_id=1, source_target_pairs={{0,4},{4,8},{8,12},{12,16},{16,20},{20,24},{24,28},{28,32},{32,36}... | collective-permute-start | bytes 49160 | tf_op jit(solution)/shard_map/ppermute | solution.py:14
  39.8 16.1 %collective-permute-start.13 = (bf16[1,32,256]{2,1,0:T(8,128)(2,1)S(1)}, bf16[1,32,256]{2,1,0:T(8,128)(2,1)S(1)}, u32[]{:S(2)}, u32[]{:S(2)}) collective-permute-start(bf16[1,32,256]{2,1,0:T(8,128)(2,1)S(1)} %get-tuple-element.10), channel_id=1, source_target_pairs={{4,0},{8,4},{12,8},{16,12},{20,16},{24,20},{28,24},{32,28},{36,32}... | collective-permute-start | bytes 49160 | tf_op jit(solution)/shard_map/ppermute | solution.py:17
  57.3 3.9 collective-permute-start.2
  61.3 8.6 %all_gather.14 = bf16[512,256]{0,1:T(8,128)(2,1)S(1)} all-gather(bf16[512,64]{0,1:T(8,128)(2,1)S(1)} %copy-done.7), channel_id=1, replica_groups=mesh['rows'=128,'cols'=4] {'cols'}, dimensions={1}, use_global_device_ids=true | all-gather | bytes 327680 | tf_op jit(solution)/shard_map/all_gather | solution.py:64
  74.4 2.1 collective-permute-start.3
  76.5 3.4 collective-permute-done.3
  80.1 1.9 collective-permute-start.14
  82.0 2.4 collective-permute-start.15
  84.5 29.8 %all-gather.5.cloned.1.call-done = bf16[2,4608,512]{2,1,0:T(8,128)(2,1)} async-done(((bf16[2,4608,128]{2,1,0:T(8,128)(2,1)}), bf16[2,4608,512]{2,1,0:T(8,128)(2,1)}) %all-gather.5.cloned.1.call-update) | async-done | bytes 9437200 | tf_op jit(solution)/shard_map/all_gather | solution.py:48
  114.4 5.0 fusion.11
  119.4 2.4 collective-permute-start.4
  121.8 1.3 collective-permute-start.5
  123.1 3.1 collective-permute-done.5
  126.2 3.1 collective-permute-start.6
  129.3 1.9 collective-permute-start.7
  131.3 3.0 collective-permute-done.7
  134.4 38.2 %all-gather.9.cloned.1.call-done = bf16[4608,512]{1,0:T(8,128)(2,1)} async-done(((bf16[4608,128]{1,0:T(8,128)(2,1)}), bf16[4608,512]{1,0:T(8,128)(2,1)}) %all-gather.9.cloned.1.call-update) | async-done | bytes 4718608 | tf_op jit(solution)/shard_map/all_gather | solution.py:48
  172.6 3.7 fusion.44
  177.2 3.1 collective-permute-start.8
  180.3 1.3 collective-permute-start.9
  181.7 3.1 collective-permute-done.9
  184.8 3.1 collective-permute-start.10
  187.9 1.9 collective-permute-start.11
  189.9 3.4 collective-permute-done.11
  195.2 372.2 %fusion = f32[24,256]{1,0:T(8,128)S(1)} fusion(f32[2304,256]{1,0:T(8,128)S(1)} %fusion.5), kind=kCustom, calls=%all-reduce-scatter | all-reduce-scatter fusion | flops 786433 | bytes 2385920
  567.4 2.6 collective-permute-start.16
  570.0 1.3 collective-permute-start.47
  572.1 65.4 %collective-permute-start.17 = (f32[24,256]{1,0:T(8,128)S(1)}, f32[24,256]{1,0:T(8,128)S(1)}, u32[]{:S(2)}, u32[]{:S(2)}) collective-permute-start(f32[24,256]{1,0:T(8,128)S(1)} %fusion), channel_id=1, source_target_pairs={{0,8},{4,12},{8,16},{12,20},{16,24},{20,28},{24,32},{28,36},{32,40... | collective-permute-start | bytes 73736
  637.5 4.5 collective-permute-start.18
  642.0 5.0 collective-permute-start.19
  647.0 6.1 collective-permute-start.20
  653.1 4.4 collective-permute-start.21
  658.2 7.7 %collective-permute-start.22 = (f32[24,256]{1,0:T(8,128)S(1)}, f32[24,256]{1,0:T(8,128)S(1)}, u32[]{:S(2)}, u32[]{:S(2)}) collective-permute-start(f32[24,256]{1,0:T(8,128)S(1)} %fusion), channel_id=1, source_target_pairs={{0,28},{4,32},{8,36},{12,40},{16,44},{20,48},{24,52},{28,56},{32,6... | collective-permute-start | bytes 73736
  666.0 3.0 collective-permute-start.23
  669.0 7.5 collective-permute-start.24
  676.5 4.2 collective-permute-start.25
  680.7 8.5 %collective-permute-start.26 = (f32[24,256]{1,0:T(8,128)S(1)}, f32[24,256]{1,0:T(8,128)S(1)}, u32[]{:S(2)}, u32[]{:S(2)}) collective-permute-start(f32[24,256]{1,0:T(8,128)S(1)} %fusion), channel_id=1, source_target_pairs={{0,44},{4,48},{8,52},{12,56},{16,60},{20,64},{24,68},{28,72},{32,7... | collective-permute-start | bytes 73736
  689.9 5.1 collective-permute-start.27
  695.0 2.8 collective-permute-start.28
  697.8 2.3 collective-permute-start.29
  700.1 4.0 collective-permute-start.30
  704.2 2.3 collective-permute-start.31
  707.1 1.6 copy.16
  708.7 1.7 collective-permute-start.32
  710.4 3.4 collective-permute-start.33
  713.9 2.9 collective-permute-start.34
  716.8 1.3 collective-permute-start.35
  718.1 1.8 collective-permute-start.36
  720.8 2.3 collective-permute-start.37
  723.1 3.5 collective-permute-start.38
  726.6 1.3 collective-permute-start.39
  728.0 2.2 collective-permute-start.40
  730.2 3.1 collective-permute-start.41
  733.3 2.6 convolution_convert_fusion
  735.8 1.6 collective-permute-start.42
  737.4 1.3 collective-permute-start.43
  738.7 1.3 collective-permute-start.44
  740.0 2.1 collective-permute-start.45
  742.2 1.6 collective-permute-start.46
  745.0 4.3 concatenate.124
  749.4 15.1 %psum.7 = f32[18,256]{1,0:T(8,128)} all-reduce(f32[18,256]{1,0:T(8,128)S(1)} %constant_dynamic-slice_fusion), channel_id=1, replica_groups=mesh['rows'=128,'cols'=4] {'cols'}, use_global_device_ids=true, to_apply=%region_1.2 | all-reduce | flops 4608 | bytes 36864 | tf_op jit(solution)/shard_map/psum | solution.py:101
  (137 shorter events, 11.7 us)
Async XLA Ops:
  7.2 107.2 %all-gather.5.cloned.1.call-start = ((), (), s32[]{:S(2)}) async-start(), calls=%async_computation | async-start | bytes 11796480 | tf_op jit(solution)/shard_map/all_gather | solution.py:48
  10.5 0.8 copy-start.8
  10.5 2.1 copy-start.5
  10.5 7.4 copy-start.1
  10.5 50.8 %copy-start.7 = (bf16[512,64]{0,1:T(8,128)(2,1)S(1)}, bf16[512,64]{0,1:T(8,128)(2,1)}, u32[]{:S(2)}) copy-start(bf16[512,64]{0,1:T(8,128)(2,1)} %param.10) | copy-start | bytes 196612
  10.5 162.1 %all-gather.9.cloned.1.call-start = ((), (), s32[]{:S(2)}) async-start(), calls=%async_computation.2 | async-start | bytes 5898240 | tf_op jit(solution)/shard_map/all_gather | solution.py:48
  11.3 695.9 %all-gather.7.cloned.1.call-start = ((), (), s32[]{:S(2)}) async-start(), calls=%async_computation.1 | async-start | bytes 1474560 | tf_op jit(solution)/shard_map/all_gather | solution.py:63
  12.7 44.6 %collective-permute-start = (bf16[1,8,512]{2,1,0:T(8,128)(2,1)S(1)}, bf16[1,8,512]{2,1,0:T(8,128)(2,1)S(1)}, u32[]{:S(2)}, u32[]{:S(2)}) collective-permute-start(bf16[1,8,512]{2,1,0:T(8,128)(2,1)S(1)} %get-tuple-element.20), channel_id=1, source_target_pairs={{0,4},{4,8},{8,12},{12,16},{16,20},{20,24},{24,28},{28,32},{32,36}... | collective-permute-start | bytes 24584 | tf_op jit(solution)/shard_map/ppermute | solution.py:14
  16.6 40.7 %collective-permute-start.1 = (bf16[1,8,512]{2,1,0:T(8,128)(2,1)S(1)}, bf16[1,8,512]{2,1,0:T(8,128)(2,1)S(1)}, u32[]{:S(2)}, u32[]{:S(2)}) collective-permute-start(bf16[1,8,512]{2,1,0:T(8,128)(2,1)S(1)} %get-tuple-element.21), channel_id=1, source_target_pairs={{4,0},{8,4},{12,8},{16,12},{20,16},{24,20},{28,24},{32,28},{36,32}... | collective-permute-start | bytes 24584 | tf_op jit(solution)/shard_map/ppermute | solution.py:17
  17.9 62.1 %collective-permute-start.12 = (bf16[1,32,256]{2,1,0:T(8,128)(2,1)S(1)}, bf16[1,32,256]{2,1,0:T(8,128)(2,1)S(1)}, u32[]{:S(2)}, u32[]{:S(2)}) collective-permute-start(bf16[1,32,256]{2,1,0:T(8,128)(2,1)S(1)} %get-tuple-element.11), channel_id=1, source_target_pairs={{0,4},{4,8},{8,12},{12,16},{16,20},{20,24},{24,28},{28,32},{32,36}... | collective-permute-start | bytes 49160 | tf_op jit(solution)/shard_map/ppermute | solution.py:14
  39.8 40.2 %collective-permute-start.13 = (bf16[1,32,256]{2,1,0:T(8,128)(2,1)S(1)}, bf16[1,32,256]{2,1,0:T(8,128)(2,1)S(1)}, u32[]{:S(2)}, u32[]{:S(2)}) collective-permute-start(bf16[1,32,256]{2,1,0:T(8,128)(2,1)S(1)} %get-tuple-element.10), channel_id=1, source_target_pairs={{4,0},{8,4},{12,8},{16,12},{20,16},{24,20},{28,24},{32,28},{36,32}... | collective-permute-start | bytes 49160 | tf_op jit(solution)/shard_map/ppermute | solution.py:17
  57.3 19.1 %collective-permute-start.2 = (bf16[4,1,512]{2,1,0:T(2,128)(2,1)S(1)}, bf16[4,1,512]{2,1,0:T(2,128)(2,1)S(1)}, u32[]{:S(2)}, u32[]{:S(2)}) collective-permute-start(bf16[4,1,512]{2,1,0:T(2,128)(2,1)S(1)} %get-tuple-element.17), channel_id=1, source_target_pairs={{0,1},{1,2},{2,3},{4,5},{5,6},{6,7},{8,9},{9,10},{10,11},{12,13},{... | collective-permute-start | bytes 12296 | tf_op jit(solution)/shard_map/ppermute | solution.py:14
  74.4 5.5 collective-permute-start.3
  80.1 4.4 collective-permute-start.14
  82.0 47.2 %collective-permute-start.15 = (bf16[10,1,256]{2,1,0:T(2,128)(2,1)S(1)}, bf16[10,1,256]{2,1,0:T(2,128)(2,1)S(1)}, u32[]{:S(2)}, u32[]{:S(2)}) collective-permute-start(bf16[10,1,256]{2,1,0:T(2,128)(2,1)S(1)} %get-tuple-element.4), channel_id=1, source_target_pairs={{1,0},{2,1},{3,2},{5,4},{6,5},{7,6},{9,8},{10,9},{11,10},{13,12},{... | collective-permute-start | bytes 15368 | tf_op jit(solution)/shard_map/ppermute | solution.py:17
  119.4 3.7 collective-permute-start.4
  121.8 4.4 collective-permute-start.5
  126.2 5.1 collective-permute-start.6
  129.3 5.0 collective-permute-start.7
  176.3 0.9 copy-start.6
  177.2 4.5 collective-permute-start.8
  180.3 4.5 collective-permute-start.9
  184.8 5.0 collective-permute-start.10
  187.9 5.4 collective-permute-start.11
  189.9 3.7 copy-start.2
  193.6 1.1 copy-start.3
  567.4 85.7 %collective-permute-start.16 = (f32[24,256]{1,0:T(8,128)S(1)}, f32[24,256]{1,0:T(8,128)S(1)}, u32[]{:S(2)}, u32[]{:S(2)}) collective-permute-start(f32[24,256]{1,0:T(8,128)S(1)} %fusion), channel_id=1, source_target_pairs={{0,4},{4,8},{8,12},{12,16},{16,20},{20,24},{24,28},{28,32},{32,36}... | collective-permute-start | bytes 73736
  570.0 76.9 %collective-permute-start.47 = (f32[18,256]{1,0:T(8,128)S(1)}, f32[18,256]{1,0:T(8,128)S(1)}, u32[]{:S(2)}, u32[]{:S(2)}) collective-permute-start(f32[18,256]{1,0:T(8,128)S(1)} %slice.277), channel_id=1, source_target_pairs={{0,128},{4,132},{8,136},{12,140},{16,144},{20,148},{24,152},{28,15... | collective-permute-start | bytes 55304
  572.1 86.1 %collective-permute-start.17 = (f32[24,256]{1,0:T(8,128)S(1)}, f32[24,256]{1,0:T(8,128)S(1)}, u32[]{:S(2)}, u32[]{:S(2)}) collective-permute-start(f32[24,256]{1,0:T(8,128)S(1)} %fusion), channel_id=1, source_target_pairs={{0,8},{4,12},{8,16},{12,20},{16,24},{20,28},{24,32},{28,36},{32,40... | collective-permute-start | bytes 73736
  637.5 28.5 %collective-permute-start.18 = (f32[24,256]{1,0:T(8,128)S(1)}, f32[24,256]{1,0:T(8,128)S(1)}, u32[]{:S(2)}, u32[]{:S(2)}) collective-permute-start(f32[24,256]{1,0:T(8,128)S(1)} %fusion), channel_id=1, source_target_pairs={{0,12},{4,16},{8,20},{12,24},{16,28},{20,32},{24,36},{28,40},{32,4... | collective-permute-start | bytes 73736
  642.0 27.0 %collective-permute-start.19 = (f32[24,256]{1,0:T(8,128)S(1)}, f32[24,256]{1,0:T(8,128)S(1)}, u32[]{:S(2)}, u32[]{:S(2)}) collective-permute-start(f32[24,256]{1,0:T(8,128)S(1)} %fusion), channel_id=1, source_target_pairs={{0,16},{4,20},{8,24},{12,28},{16,32},{20,36},{24,40},{28,44},{32,4... | collective-permute-start | bytes 73736
  647.0 29.5 %collective-permute-start.20 = (f32[24,256]{1,0:T(8,128)S(1)}, f32[24,256]{1,0:T(8,128)S(1)}, u32[]{:S(2)}, u32[]{:S(2)}) collective-permute-start(f32[24,256]{1,0:T(8,128)S(1)} %fusion), channel_id=1, source_target_pairs={{0,20},{4,24},{8,28},{12,32},{16,36},{20,40},{24,44},{28,48},{32,5... | collective-permute-start | bytes 73736
  653.1 27.6 %collective-permute-start.21 = (f32[24,256]{1,0:T(8,128)S(1)}, f32[24,256]{1,0:T(8,128)S(1)}, u32[]{:S(2)}, u32[]{:S(2)}) collective-permute-start(f32[24,256]{1,0:T(8,128)S(1)} %fusion), channel_id=1, source_target_pairs={{0,24},{4,28},{8,32},{12,36},{16,40},{20,44},{24,48},{28,52},{32,5... | collective-permute-start | bytes 73736
  658.2 31.7 %collective-permute-start.22 = (f32[24,256]{1,0:T(8,128)S(1)}, f32[24,256]{1,0:T(8,128)S(1)}, u32[]{:S(2)}, u32[]{:S(2)}) collective-permute-start(f32[24,256]{1,0:T(8,128)S(1)} %fusion), channel_id=1, source_target_pairs={{0,28},{4,32},{8,36},{12,40},{16,44},{20,48},{24,52},{28,56},{32,6... | collective-permute-start | bytes 73736
  666.0 29.1 %collective-permute-start.23 = (f32[24,256]{1,0:T(8,128)S(1)}, f32[24,256]{1,0:T(8,128)S(1)}, u32[]{:S(2)}, u32[]{:S(2)}) collective-permute-start(f32[24,256]{1,0:T(8,128)S(1)} %fusion), channel_id=1, source_target_pairs={{0,32},{4,36},{8,40},{12,44},{16,48},{20,52},{24,56},{28,60},{32,6... | collective-permute-start | bytes 73736
  669.0 28.8 %collective-permute-start.24 = (f32[24,256]{1,0:T(8,128)S(1)}, f32[24,256]{1,0:T(8,128)S(1)}, u32[]{:S(2)}, u32[]{:S(2)}) collective-permute-start(f32[24,256]{1,0:T(8,128)S(1)} %fusion), channel_id=1, source_target_pairs={{0,36},{4,40},{8,44},{12,48},{16,52},{20,56},{24,60},{28,64},{32,6... | collective-permute-start | bytes 73736
  676.5 23.7 %collective-permute-start.25 = (f32[24,256]{1,0:T(8,128)S(1)}, f32[24,256]{1,0:T(8,128)S(1)}, u32[]{:S(2)}, u32[]{:S(2)}) collective-permute-start(f32[24,256]{1,0:T(8,128)S(1)} %fusion), channel_id=1, source_target_pairs={{0,40},{4,44},{8,48},{12,52},{16,56},{20,60},{24,64},{28,68},{32,7... | collective-permute-start | bytes 73736
  680.7 23.4 %collective-permute-start.26 = (f32[24,256]{1,0:T(8,128)S(1)}, f32[24,256]{1,0:T(8,128)S(1)}, u32[]{:S(2)}, u32[]{:S(2)}) collective-permute-start(f32[24,256]{1,0:T(8,128)S(1)} %fusion), channel_id=1, source_target_pairs={{0,44},{4,48},{8,52},{12,56},{16,60},{20,64},{24,68},{28,72},{32,7... | collective-permute-start | bytes 73736
  689.9 18.8 %collective-permute-start.27 = (f32[24,256]{1,0:T(8,128)S(1)}, f32[24,256]{1,0:T(8,128)S(1)}, u32[]{:S(2)}, u32[]{:S(2)}) collective-permute-start(f32[24,256]{1,0:T(8,128)S(1)} %fusion), channel_id=1, source_target_pairs={{0,48},{4,52},{8,56},{12,60},{16,64},{20,68},{24,72},{28,76},{32,8... | collective-permute-start | bytes 73736
  695.0 15.4 %collective-permute-start.28 = (f32[24,256]{1,0:T(8,128)S(1)}, f32[24,256]{1,0:T(8,128)S(1)}, u32[]{:S(2)}, u32[]{:S(2)}) collective-permute-start(f32[24,256]{1,0:T(8,128)S(1)} %fusion), channel_id=1, source_target_pairs={{0,52},{4,56},{8,60},{12,64},{16,68},{20,72},{24,76},{28,80},{32,8... | collective-permute-start | bytes 73736
  697.8 16.0 %collective-permute-start.29 = (f32[24,256]{1,0:T(8,128)S(1)}, f32[24,256]{1,0:T(8,128)S(1)}, u32[]{:S(2)}, u32[]{:S(2)}) collective-permute-start(f32[24,256]{1,0:T(8,128)S(1)} %fusion), channel_id=1, source_target_pairs={{0,56},{4,60},{8,64},{12,68},{16,72},{20,76},{24,80},{28,84},{32,8... | collective-permute-start | bytes 73736
  700.1 16.7 %collective-permute-start.30 = (f32[24,256]{1,0:T(8,128)S(1)}, f32[24,256]{1,0:T(8,128)S(1)}, u32[]{:S(2)}, u32[]{:S(2)}) collective-permute-start(f32[24,256]{1,0:T(8,128)S(1)} %fusion), channel_id=1, source_target_pairs={{0,60},{4,64},{8,68},{12,72},{16,76},{20,80},{24,84},{28,88},{32,9... | collective-permute-start | bytes 73736
  704.2 14.0 %collective-permute-start.31 = (f32[24,256]{1,0:T(8,128)S(1)}, f32[24,256]{1,0:T(8,128)S(1)}, u32[]{:S(2)}, u32[]{:S(2)}) collective-permute-start(f32[24,256]{1,0:T(8,128)S(1)} %fusion), channel_id=1, source_target_pairs={{0,64},{4,68},{8,72},{12,76},{16,80},{20,84},{24,88},{28,92},{32,9... | collective-permute-start | bytes 73736
  708.7 12.1 %collective-permute-start.32 = (f32[24,256]{1,0:T(8,128)S(1)}, f32[24,256]{1,0:T(8,128)S(1)}, u32[]{:S(2)}, u32[]{:S(2)}) collective-permute-start(f32[24,256]{1,0:T(8,128)S(1)} %fusion), channel_id=1, source_target_pairs={{0,68},{4,72},{8,76},{12,80},{16,84},{20,88},{24,92},{28,96},{32,1... | collective-permute-start | bytes 73736
  710.4 12.6 %collective-permute-start.33 = (f32[24,256]{1,0:T(8,128)S(1)}, f32[24,256]{1,0:T(8,128)S(1)}, u32[]{:S(2)}, u32[]{:S(2)}) collective-permute-start(f32[24,256]{1,0:T(8,128)S(1)} %fusion), channel_id=1, source_target_pairs={{0,72},{4,76},{8,80},{12,84},{16,88},{20,92},{24,96},{28,100},{32,... | collective-permute-start | bytes 73736
  713.9 12.8 %collective-permute-start.34 = (f32[24,256]{1,0:T(8,128)S(1)}, f32[24,256]{1,0:T(8,128)S(1)}, u32[]{:S(2)}, u32[]{:S(2)}) collective-permute-start(f32[24,256]{1,0:T(8,128)S(1)} %fusion), channel_id=1, source_target_pairs={{0,76},{4,80},{8,84},{12,88},{16,92},{20,96},{24,100},{28,104},{32... | collective-permute-start | bytes 73736
  716.8 11.1 %collective-permute-start.35 = (f32[24,256]{1,0:T(8,128)S(1)}, f32[24,256]{1,0:T(8,128)S(1)}, u32[]{:S(2)}, u32[]{:S(2)}) collective-permute-start(f32[24,256]{1,0:T(8,128)S(1)} %fusion), channel_id=1, source_target_pairs={{0,80},{4,84},{8,88},{12,92},{16,96},{20,100},{24,104},{28,108},{3... | collective-permute-start | bytes 73736
  718.1 12.0 %collective-permute-start.36 = (f32[24,256]{1,0:T(8,128)S(1)}, f32[24,256]{1,0:T(8,128)S(1)}, u32[]{:S(2)}, u32[]{:S(2)}) collective-permute-start(f32[24,256]{1,0:T(8,128)S(1)} %fusion), channel_id=1, source_target_pairs={{0,84},{4,88},{8,92},{12,96},{16,100},{20,104},{24,108},{28,112},{... | collective-permute-start | bytes 73736
  720.8 15.1 %collective-permute-start.37 = (f32[24,256]{1,0:T(8,128)S(1)}, f32[24,256]{1,0:T(8,128)S(1)}, u32[]{:S(2)}, u32[]{:S(2)}) collective-permute-start(f32[24,256]{1,0:T(8,128)S(1)} %fusion), channel_id=1, source_target_pairs={{0,88},{4,92},{8,96},{12,100},{16,104},{20,108},{24,112},{28,116},... | collective-permute-start | bytes 73736
  723.1 14.4 %collective-permute-start.38 = (f32[24,256]{1,0:T(8,128)S(1)}, f32[24,256]{1,0:T(8,128)S(1)}, u32[]{:S(2)}, u32[]{:S(2)}) collective-permute-start(f32[24,256]{1,0:T(8,128)S(1)} %fusion), channel_id=1, source_target_pairs={{0,92},{4,96},{8,100},{12,104},{16,108},{20,112},{24,116},{28,120}... | collective-permute-start | bytes 73736
  726.6 12.1 %collective-permute-start.39 = (f32[24,256]{1,0:T(8,128)S(1)}, f32[24,256]{1,0:T(8,128)S(1)}, u32[]{:S(2)}, u32[]{:S(2)}) collective-permute-start(f32[24,256]{1,0:T(8,128)S(1)} %fusion), channel_id=1, source_target_pairs={{0,96},{4,100},{8,104},{12,108},{16,112},{20,116},{24,120},{28,124... | collective-permute-start | bytes 73736
  728.0 12.1 %collective-permute-start.40 = (f32[24,256]{1,0:T(8,128)S(1)}, f32[24,256]{1,0:T(8,128)S(1)}, u32[]{:S(2)}, u32[]{:S(2)}) collective-permute-start(f32[24,256]{1,0:T(8,128)S(1)} %fusion), channel_id=1, source_target_pairs={{0,100},{4,104},{8,108},{12,112},{16,116},{20,120},{24,124},{28,12... | collective-permute-start | bytes 73736
  730.2 12.0 %collective-permute-start.41 = (f32[24,256]{1,0:T(8,128)S(1)}, f32[24,256]{1,0:T(8,128)S(1)}, u32[]{:S(2)}, u32[]{:S(2)}) collective-permute-start(f32[24,256]{1,0:T(8,128)S(1)} %fusion), channel_id=1, source_target_pairs={{0,104},{4,108},{8,112},{12,116},{16,120},{20,124},{24,128},{28,13... | collective-permute-start | bytes 73736
  733.3 10.5 %copy-start = (bf16[2304,256]{0,1:T(8,128)(2,1)S(1)}, bf16[2304,256]{0,1:T(8,128)(2,1)}, u32[]{:S(2)}) copy-start(bf16[2304,256]{0,1:T(8,128)(2,1)} %all-gather.7.cloned.1.call-done) | copy-start | bytes 3538948
  733.3 10.5 %copy-start.4 = (bf16[8,32,2304]{2,1,0:T(8,128)(2,1)S(1)}, bf16[8,32,2304]{2,1,0:T(8,128)(2,1)}, u32[]{:S(2)}) copy-start(bf16[8,32,2304]{2,1,0:T(8,128)(2,1)} %copy-done.3) | copy-start | bytes 3538948
  735.8 9.1 %collective-permute-start.42 = (f32[24,256]{1,0:T(8,128)S(1)}, f32[24,256]{1,0:T(8,128)S(1)}, u32[]{:S(2)}, u32[]{:S(2)}) collective-permute-start(f32[24,256]{1,0:T(8,128)S(1)} %fusion), channel_id=1, source_target_pairs={{0,108},{4,112},{8,116},{12,120},{16,124},{20,128},{24,132},{28,13... | collective-permute-start | bytes 73736
  737.4 7.6 collective-permute-start.43
  738.7 6.2 collective-permute-start.44
  740.0 4.9 collective-permute-start.45
  742.2 2.8 collective-permute-start.46
Sparse Core Ops, SparseCore 0:
  10.6 103.7 all-gather.4
  116.4 56.1 all-gather.8
  174.7 27.5 all-gather.6
where the time goes:
time: 773 us; the launch traced here: 771 us
  blocking collectives  396 us (51%)
  starting transfers between devices  240 us (31%)
  waiting for transfers between devices  84.9 us (11%)
  between operations  19.5 us (3%)
  matrix products  13 us (2%)
  local copies, waits for them, and re-layouts  11.2 us (1%)
    unnamed x1, blocking collectives  372 us
    unnamed x32, starting transfers between devices  168 us
    all_gather x2, waiting for transfers between devices, mid_terms(): lax.all_gather(stacked, 'cols', axis=2, tiled=True)  68 us
    ppermute x8, starting transfers between devices, extended(): lax.ppermute(lax.slice_in_dim(block, block.shape[dim] - width, None, axis...  43.3 us
    ppermute x8, starting transfers between devices, extended(): lax.ppermute(lax.slice_in_dim(block, 0, width, axis=dim), axis, backward)  28.3 us
    ppermute x8, waiting for transfers between devices, extended(): lax.ppermute(lax.slice_in_dim(block, 0, width, axis=dim), axis, backward)  16 us
  transfers between devices with their start and end apart: 51, of which 7 were waited for; matrix products, arithmetic and copies ran while one was open for 51% of the time, Pallas kernels for 0%

commit v1 on v0

v1 whole, which is shorter than its diff:
```python
import math

import jax
import jax.numpy as jnp
import numpy as np
from jax import lax
from jax.experimental import pallas as pl
from jax.experimental.pallas import tpu as pltpu
from jax.sharding import PartitionSpec as P

BF = jnp.bfloat16
F32 = jnp.float32
MIB = 1024 * 1024


def call(body, outs, scratch, flops, vmem, name, n_in):
    return pl.pallas_call(
        body,
        out_shape=outs,
        in_specs=[pl.BlockSpec(memory_space=pltpu.VMEM)] * n_in,
        out_specs=[pl.BlockSpec(memory_space=pltpu.VMEM)] * len(outs),
        scratch_shapes=scratch,
        compiler_params=pltpu.CompilerParams(vmem_limit_bytes=vmem * MIB),
        cost_estimate=pl.CostEstimate(flops=flops, bytes_accessed=4 * MIB, transcendentals=0),
        name=name,
    )


def shape(dims, kind):
    return jax.ShapeDtypeStruct(dims, kind)


def silu(value):
    return value * (1.0 / (1.0 + jnp.exp(-value)))


def shifted(field, step):
    if step == 0:
        return field
    edge = jnp.zeros((field.shape[0], 1, field.shape[2]), field.dtype)
    if step < 0:
        return jnp.concatenate([edge, field[:, :-1]], axis=1)
    return jnp.concatenate([field[:, 1:], edge], axis=1)


def pack_kernel(fine_ref, cot_ref, weight_ref, proj_ref, mid_ref, bulk_ref, down_ref, up_ref, own_ref):
    bulk_ref[0:256, :] = fine_ref[...]
    bulk_ref[256:512, :] = cot_ref[...]
    for tap in range(9):
        base = tap * 256
        bulk_ref[512 + 64 * tap : 576 + 64 * tap, :] = jnp.concatenate(
            [weight_ref[base + 64 * q : base + 64 * q + 64, :] for q in range(4)], axis=1
        )
    bulk_ref[1088:1216, :] = jnp.concatenate(
        [proj_ref[128 * q : 128 * q + 128, :] for q in range(4)], axis=1
    )
    low, high = mid_ref[:, 0:256], mid_ref[:, 256:512]
    for ref in (down_ref, up_ref, own_ref):
        ref[0:16, :] = low
        ref[16:32, :] = high
    down_ref[32:64, :] = cot_ref[224:256, :]
    up_ref[32:64, :] = cot_ref[0:32, :]


def first_kernel(near_ref, teacher_ref, student_ref, coef_ref, sec_ref, mid_ref, base_ref, raw_ref, in_ref):
    row, col = lax.axis_index("rows"), lax.axis_index("cols")
    last = lax.axis_size("rows") - 1
    tiles = [near_ref[s].astype(F32) for s in range(4)]
    lines = []
    for start, half in ((0, 0), (0, 8), (128, 0), (128, 8), (64, 0), (64, 8)):
        at = start + half
        lines.append(
            jnp.concatenate(
                [jnp.concatenate([t[at : at + 8], t[at + 16 : at + 24]], axis=1) for t in tiles], axis=0
            )
        )
    raw = jnp.stack(lines)
    raw_ref[...] = raw.reshape(192, 512)
    lit = silu(raw + coef_ref[0:1, :].reshape(1, 1, 512))
    line = lax.broadcasted_iota(jnp.int32, (6, 32, 512), 0)
    inside = ((line >= 2) | (row > 0)) & ((line < 4) | (row < last))
    lit = jnp.where(inside, lit, 0.0)
    for at, step in enumerate((-1, 0, 1)):
        in_ref[at] = shifted(lit, step).astype(BF).reshape(192, 512)
    total = jnp.zeros((128, 256), F32)
    for dy in range(3):
        for dx in range(3):
            k = (3 * dy + dx) * 512
            both = jnp.concatenate([teacher_ref[k : k + 512, :], student_ref[k : k + 512, :]], axis=1)
            total += jnp.dot(in_ref[dx, 32 * dy : 32 * dy + 128, :], both, preferred_element_type=F32)
    own = pl.ds(pl.multiple_of(col * 128, 128), 128)
    anchor = raw_ref[32:160, own]
    one, two = coef_ref[2:3, 0:128], coef_ref[3:4, 0:128]
    middle = anchor + one * total[:, 0:128]
    second = silu(middle + coef_ref[1:2, own])
    line = lax.broadcasted_iota(jnp.int32, (128, 128), 0)
    inside = ((line >= 32) | (row > 0)) & ((line < 96) | (row < last))
    sec_ref[...] = jnp.where(inside, second, 0.0).astype(BF)
    mid_ref[...] = middle[32:96]
    base_ref[...] = anchor[32:96] + (one + two) * total[32:96, 128:256]


def second_kernel(sec_ref, teacher_ref, mid_ref, base_ref, coef_ref, out_ref, in_ref):
    field = jnp.concatenate([sec_ref[s] for s in range(4)], axis=1).astype(F32).reshape(4, 32, 512)
    for at, step in enumerate((-1, 0, 1)):
        in_ref[at] = shifted(field, step).astype(BF).reshape(128, 512)
    total = jnp.zeros((64, 128), F32)
    for dy in range(3):
        for dx in range(3):
            k = (3 * dy + dx) * 512
            total += jnp.dot(
                in_ref[dx, 32 * dy : 32 * dy + 64, :], teacher_ref[k : k + 512, :], preferred_element_type=F32
            )
    target = mid_ref[...] + coef_ref[3:4, 0:128] * total
    out_ref[0:64, :] = target.astype(BF)
    out_ref[64:128, :] = (target - base_ref[...]).astype(BF)


def grad_kernel(bulk_ref, near_ref, late_ref, part_ref, field_ref, gap_ref, sum_ref, gap_scratch):
    col = lax.axis_index("cols")
    target = jnp.concatenate([late_ref[s, 0:64, :] for s in range(4)], axis=1)
    place = lax.broadcasted_iota(jnp.int32, (128, 32), 0) // 4
    repeat = (place == lax.broadcasted_iota(jnp.int32, (128, 32), 1)).astype(BF)
    proj = jnp.concatenate(
        [
            jnp.concatenate([bulk_ref[s, 1088:1216, 64 * q : 64 * q + 64] for s in range(4)], axis=1)
            for q in range(4)
        ],
        axis=0,
    )
    for m in range(2):
        wide = jnp.dot(repeat, target[32 * m : 32 * m + 32], preferred_element_type=F32).astype(BF)
        lifted = jnp.dot(wide, proj, preferred_element_type=F32)
        for i in range(4 * m, 4 * m + 4):
            noisy = jnp.concatenate([bulk_ref[s, 32 * i : 32 * i + 32, :] for s in range(4)], axis=0)
            field_ref[128 * i : 128 * i + 128, :] = (noisy.astype(F32) + lifted).astype(BF)
    pair = pl.ds(pl.multiple_of((col // 2) * 128, 128), 128)
    lines = [near_ref[s, 32:64, pair] for s in range(4)]
    for i in range(8):
        lines += [bulk_ref[s, 256 + 32 * i : 288 + 32 * i, pair] for s in range(4)]
    lines += [near_ref[s, 96:128, pair] for s in range(4)]
    cot = jnp.concatenate(lines, axis=0).astype(F32)
    cot = jnp.where(col % 2 == 1, cot[:, 64:128], cot[:, 0:64]).reshape(10, 128, 64)
    moved = jnp.concatenate([shifted(cot, -dx) for dx in (-1, 0, 1)], axis=2).astype(BF).reshape(1280, 192)
    field = field_ref[...]
    for dy in (-1, 0, 1):
        term = lax.dot_general(
            field,
            moved[(1 - dy) * 128 : (1 - dy) * 128 + 1024],
            (((0,), (0,)), ((), ())),
            preferred_element_type=F32,
        )
        for dx in range(3):
            one = term[:, 64 * dx : 64 * dx + 64]
            at = (3 * (dy + 1) + dx) * 256
            sum_ref[at : at + 256, :] = jnp.concatenate([one, one], axis=1)
    owners, width = part_ref.shape
    each = 2304 // owners
    lane = lax.broadcasted_iota(jnp.int32, (owners, 128), 1)
    for j in range(width // 128):
        even = sum_ref[pl.ds(2 * j, owners, stride=each), :]
        odd = sum_ref[pl.ds(2 * j + 1, owners, stride=each), :]
        part_ref[:, 128 * j : 128 * j + 128] = jnp.where(lane < 64, even, odd).astype(BF)
    gap_scratch[...] = jnp.concatenate([late_ref[s, 64:128, :] for s in range(4)], axis=1).astype(F32)
    gap_ref[...] = jnp.concatenate(
        [gap_scratch[pl.ds(pl.multiple_of(32 * i + 8 * col, 8), 8), :] for i in range(2)], axis=0
    ).astype(BF)


def fine_kernel(bulk_ref, near_ref, field_ref, above_ref, below_ref, out_ref, back_ref, weight_ref, in_ref):
    col = lax.axis_index("cols")
    for tap in range(9):
        at = 512 + 64 * tap
        for q in range(4):
            weight_ref[256 * tap + 64 * q : 256 * tap + 64 * q + 64, :] = jnp.concatenate(
                [bulk_ref[s, at : at + 64, 64 * q : 64 * q + 64] for s in range(4)], axis=1
            )
    start = pl.multiple_of(32 * col, 32)
    before = pl.multiple_of(jnp.maximum(32 * col - 16, 0), 16)
    after = pl.multiple_of(jnp.minimum(32 * col + 32, 112), 16)

    def window(ref, base):
        left = ref[pl.ds(base + before, 16), :].astype(F32)
        right = ref[pl.ds(base + after, 16), :].astype(F32)
        return jnp.concatenate(
            [
                jnp.where(col > 0, left, 0.0),
                ref[pl.ds(base + start, 32), :].astype(F32),
                jnp.where(col < 3, right, 0.0),
            ],
            axis=0,
        )

    wide = jnp.stack(
        [window(above_ref, 0)] + [window(field_ref, 128 * i) for i in range(8)] + [window(below_ref, 0)]
    )
    for at in range(3):
        in_ref[at] = wide[:, 15 + at : 47 + at].astype(BF).reshape(320, 256)
    total = jnp.zeros((256, 256), F32)
    for dy in range(3):
        for dx in range(3):
            k = (3 * dy + dx) * 256
            total += jnp.dot(
                in_ref[dx, 32 * dy : 32 * dy + 256, :], weight_ref[k : k + 256, :], preferred_element_type=F32
            )
    out_ref[...] = total.astype(BF)

    left_tile, right_tile = jnp.maximum(col - 1, 0), jnp.minimum(col + 1, 3)

    def cot_window(ref, at):
        left = ref[left_tile, at + 16 : at + 32, :].astype(F32)
        right = ref[right_tile, at : at + 16, :].astype(F32)
        return jnp.concatenate(
            [
                jnp.where(col > 0, left, 0.0),
                ref[col, at : at + 32, :].astype(F32),
                jnp.where(col < 3, right, 0.0),
            ],
            axis=0,
        )

    wide = jnp.stack(
        [cot_window(near_ref, 32)]
        + [cot_window(bulk_ref, 256 + 32 * i) for i in range(8)]
        + [cot_window(near_ref, 96)]
    )
    for at in range(3):
        in_ref[at] = wide[:, 15 + at : 47 + at].astype(BF).reshape(320, 256)
    total = jnp.zeros((256, 256), F32)
    for dy in range(3):
        for dx in range(3):
            k = (3 * dy + dx) * 256
            total += lax.dot_general(
                in_ref[2 - dx, 32 * (2 - dy) : 32 * (2 - dy) + 256, :],
                weight_ref[k : k + 256, :],
                (((1,), (1,)), ((), ())),
                preferred_element_type=F32,
            )
    back_ref[...] = total.astype(BF)


def on_device(
    fine_noisy, fine_weight, projection, mid_noisy, teacher_weight, student_weight, steps, cotangent
):
    count = lax.axis_size("rows")
    forward = [(i, i + 1) for i in range(count - 1)]
    backward = [(i + 1, i) for i in range(count - 1)]

    bulk, down, up, own = call(
        pack_kernel,
        [shape((1216, 256), BF), shape((64, 256), BF), shape((64, 256), BF), shape((32, 256), BF)],
        [],
        MIB,
        16,
        "pack",
        5,
    )(
        fine_noisy.reshape(256, 256),
        cotangent.reshape(256, 256),
        fine_weight,
        projection,
        mid_noisy.reshape(16, 512),
    )
    bulk = lax.all_gather(bulk, "cols", axis=0)
    above = lax.ppermute(down, "rows", forward)
    below = lax.ppermute(up, "rows", backward)

    freqs = jnp.asarray(np.exp(-math.log(10000.0) * np.arange(256, dtype=np.float32) / 256).astype(np.float32))
    times = steps.astype(F32)
    angles = times[0:2, None] * freqs[None, :]
    waves = jnp.concatenate([jnp.sin(angles), jnp.cos(angles)], axis=1)
    deltas = jnp.broadcast_to(((times[1:3] - times[0:2]) / 1000.0)[:, None], (2, 512))
    coef = jnp.concatenate([waves, deltas], axis=0)

    near = lax.all_gather(jnp.concatenate([above, below, own], axis=0), "cols", axis=0)
    sec, middle, base = call(
        first_kernel,
        [shape((128, 128), BF), shape((64, 128), F32), shape((64, 128), F32)],
        [pltpu.VMEM((192, 512), F32), pltpu.VMEM((3, 192, 512), BF)],
        300 * MIB,
        16,
        "first",
        4,
    )(near, teacher_weight, student_weight, coef)
    sec = lax.all_gather(sec, "cols", axis=0)
    (late,) = call(
        second_kernel,
        [shape((128, 128), BF)],
        [pltpu.VMEM((3, 128, 512), BF)],
        100 * MIB,
        16,
        "second",
        5,
    )(sec, teacher_weight, middle, base, coef)
    late = lax.all_gather(late, "cols", axis=0)
    part, field, gap = call(
        grad_kernel,
        [shape((count, 64 * 2304 // count), BF), shape((1024, 256), BF), shape((16, 512), BF)],
        [pltpu.VMEM((2304, 128), F32), pltpu.VMEM((64, 512), F32)],
        1000 * MIB,
        32,
        "grad",
        3,
    )(bulk, near, late)
    over = lax.ppermute(field[896:1024], "rows", forward)
    under = lax.ppermute(field[0:128], "rows", backward)
    part = lax.all_to_all(part, "rows", 0, 0, tiled=True)
    share = jnp.sum(part.astype(F32), axis=0) * (1.0 / math.sqrt(1024 * count))
    share = share.reshape(2304 // count, 64)
    grad_weight = lax.all_gather(share, "cols", axis=1, tiled=True)
    fine_out, grad_input = call(
        fine_kernel,
        [shape((256, 256), BF), shape((256, 256), BF)],
        [pltpu.VMEM((2304, 256), BF), pltpu.VMEM((3, 320, 256), BF)],
        1000 * MIB,
        32,
        "fine",
        5,
    )(bulk, near, field, over, under)
    return (
        fine_out.reshape(8, 32, 256),
        grad_input.reshape(8, 32, 256),
        grad_weight,
        gap.reshape(2, 8, 512),
    )


def solution(mesh):
    placed = (
        P("rows", "cols", None),
        P(None, "cols"),
        P(None, "cols"),
        P("rows", "cols", None),
        P(None, "cols"),
        P(None, "cols"),
        P(),
        P("rows", "cols", None),
    )
    return jax.shard_map(
        on_device,
        mesh=mesh,
        in_specs=placed,
        out_specs=(
            P("rows", "cols", None),
            P("rows", "cols", None),
            P("rows", None),
            P("rows", "cols", None),
        ),
        check_vma=False,
    )
```

time: 773 us -> 114 us (0.15)
  blocking collectives: 396 us -> 30.2 us
  starting transfers between devices: 240 us -> 25 us
  waiting for transfers between devices: 84.9 us -> 26.3 us
  matrix products: 13 us -> 0 us
    unnamed x1 -> x0, blocking collectives: 372 us -> none
    unnamed x32 -> x0, starting transfers between devices: 168 us -> none
    ppermute x16 -> x4, starting transfers between devices: 71.6 us -> 9.03 us  [the longest x1 3.97 us: on_device(): above = lax.ppermute(down, 'rows', forward)]
    all_gather x3 -> x1, waiting for transfers between devices: 68 us -> 12.5 us  [on_device(): bulk = lax.all_gather(bulk, 'cols', axis=0)]
    all_gather x1 -> x4, blocking collectives: 8.57 us -> 30.2 us  [the longest x1 11.1 us: on_device(): lax.all_gather(jnp.concatenate([above, below, own], axis=0), 'cols', axis=0)]
    all_to_all x0 -> x1, starting transfers between devices: none -> 15.9 us  [on_device(): part = lax.all_to_all(part, 'rows', 0, 0, tiled=True)]
    psum x1 -> x0, blocking collectives: 15.1 us -> none  [on_device(): grad_weight = lax.psum(share, 'cols')]
    dot_general x6 -> x0, matrix products: 13 us -> none  [the longest x2 8.66 us: mid_terms(): jnp.einsum('ijk,wkc->wijc', tiles, lax.all_gather(stacked, 'cols', axis=2...]
  transfers between devices with their start and end apart: 51 -> 6, of which waited for: 7 -> 5; matrix products, arithmetic and copies ran while one was open for 51% -> 0% of each run, Pallas kernels for 0% -> 2%
where the time goes in v1:
time: 114 us
  blocking collectives  30.2 us (26%)
  waiting for transfers between devices  26.3 us (23%)
  starting transfers between devices  25 us (22%)
  between operations  14.2 us (12%)
  local copies, waits for them, and re-layouts  12.1 us (11%)
  Pallas kernels  4.44 us (4%)
  other arithmetic  1.58 us (1%)
    all_to_all x1, starting transfers between devices, on_device(): part = lax.all_to_all(part, 'rows', 0, 0, tiled=True)  15.9 us
    all_gather x1, waiting for transfers between devices, on_device(): bulk = lax.all_gather(bulk, 'cols', axis=0)  12.5 us
    unnamed x25, local copies, waits for them, and re-layouts  11.4 us
    all_gather x1, blocking collectives, on_device(): lax.all_gather(jnp.concatenate([above, below, own], axis=0), 'cols', axis=0)  11.1 us
    all_gather x1, blocking collectives, on_device(): grad_weight = lax.all_gather(share, 'cols', axis=1, tiled=True)  7.04 us
    all_to_all x1, waiting for transfers between devices, on_device(): part = lax.all_to_all(part, 'rows', 0, 0, tiled=True)  6.55 us
    all_gather x1, blocking collectives, on_device(): late = lax.all_gather(late, 'cols', axis=0)  6.23 us
    all_gather x1, blocking collectives, on_device(): sec = lax.all_gather(sec, 'cols', axis=0)  5.82 us
  transfers between devices with their start and end apart: 6, of which 5 were waited for; matrix products, arithmetic and copies ran while one was open for 0% of the time, Pallas kernels for 2%

profile of v1, /device:TPU:1, one launch (start us, length us, event | category | flops | bytes accessed | tf_op | source)
XLA Modules:
  0.0 113.9 jit_solution(1476584687157616188)
XLA Ops:
  7.2 0.0 copy-start.8
  7.2 0.0 copy-start.9
  7.2 0.0 all-gather.7.cloned.1.call-start
  7.2 1.3 %copy.18.weight_ref = bf16[2304,64]{1,0:T(8,128)(2,1)S(1)} copy(bf16[2304,64]{0,1:T(8,128)(2,1)} %param.10) | data formatting | bytes 589824 | tf_op args[1]
  8.5 0.0 copy-start
  8.5 0.0 copy-start.1
  8.5 1.1 copy.19.proj_ref
  9.7 0.0 copy-start.3
  9.7 0.9 copy-done.3
  10.6 0.0 copy-start.4
  10.6 0.9 copy-done.4
  11.5 0.0 copy-start.5
  11.5 0.7 copy-done.5
  12.2 0.2 pack.1
  12.3 0.0 copy-start.2
  12.4 0.8 copy-done.2
  13.2 0.0 all-gather.7.cloned.1.call-update
  13.2 4.0 %collective-permute-start = (bf16[64,256]{1,0:T(8,128)(2,1)S(1)}, bf16[64,256]{1,0:T(8,128)(2,1)S(1)}, u32[]{:S(2)}, u32[]{:S(2)}) collective-permute-start(bf16[64,256]{1,0:T(8,128)(2,1)S(1)} %get-tuple-element.17), channel_id=1, source_target_pairs={{0,4},{4,8},{8,12},{12,16},{16,20},{20,24},{24,28},{28,32},{32,36}... | collective-permute-start | bytes 98312 | tf_op jit(solution)/shard_map/ppermute | solution.py:265
  17.2 1.3 %collective-permute-start.1 = (bf16[64,256]{1,0:T(8,128)(2,1)S(1)}, bf16[64,256]{1,0:T(8,128)(2,1)S(1)}, u32[]{:S(2)}, u32[]{:S(2)}) collective-permute-start(bf16[64,256]{1,0:T(8,128)(2,1)S(1)} %get-tuple-element.18), channel_id=1, source_target_pairs={{4,0},{8,4},{12,8},{16,12},{20,16},{24,20},{28,24},{32,28},{36,32}... | collective-permute-start | bytes 98312 | tf_op jit(solution)/shard_map/ppermute | solution.py:266
  18.5 0.0 copy-done.9
  18.5 0.1 subtract_multiply_fusion
  18.6 0.1 pad.2.clone
  18.7 0.0 copy-done.8
  18.7 0.1 multiply_sine_fusion
  18.8 0.1 maximum_maximum_fusion.coef_ref
  18.9 0.0 collective-permute-done
  18.9 3.0 %collective-permute-done.1 = bf16[64,256]{1,0:T(8,128)(2,1)S(1)} collective-permute-done((bf16[64,256]{1,0:T(8,128)(2,1)S(1)}, bf16[64,256]{1,0:T(8,128)(2,1)S(1)}, u32[]{:S(2)}, u32[]{:S(2)}) %collective-permute-start.1) | collective-permute-done | bytes 32800 | tf_op jit(solution)/shard_map/ppermute | solution.py:266
  21.8 11.1 %all-gather.1 = bf16[640,256]{1,0:T(8,128)(2,1)S(1)} all-gather(bf16[160,256]{1,0:T(8,128)(2,1)S(1)} %pad_maximum_fusion), channel_id=3, replica_groups=mesh['rows'=128,'cols'=4] {'cols'}, dimensions={0}, use_global_device_ids=true | all-gather | bytes 409600 | tf_op jit(solution)/shard_map/all_gather | solution.py:275
  33.0 0.0 copy-done
  33.0 0.0 copy-done.1
  33.0 0.5 first.1
  33.5 5.8 %all-gather.2 = bf16[512,128]{1,0:T(8,128)(2,1)S(1)} all-gather(bf16[128,128]{1,0:T(8,128)(2,1)S(1)} %get-tuple-element.20), channel_id=4, replica_groups=mesh['rows'=128,'cols'=4] {'cols'}, dimensions={0}, use_global_device_ids=true | all-gather | bytes 163840 | tf_op jit(solution)/shard_map/all_gather | solution.py:285
  39.3 0.3 second.1
  39.7 6.2 %all-gather.3 = bf16[512,128]{1,0:T(8,128)(2,1)S(1)} all-gather(bf16[128,128]{1,0:T(8,128)(2,1)S(1)} %second.1), channel_id=5, replica_groups=mesh['rows'=128,'cols'=4] {'cols'}, dimensions={0}, use_global_device_ids=true | all-gather | bytes 163840 | tf_op jit(solution)/shard_map/all_gather | solution.py:295
  45.9 12.5 %all-gather.7.cloned.1.call-done = bf16[4864,256]{1,0:T(8,128)(2,1)} async-done(((bf16[1216,256]{1,0:T(8,128)(2,1)}), bf16[4864,256]{1,0:T(8,128)(2,1)}) %all-gather.7.cloned.1.call-update) | async-done | bytes 2490384 | tf_op jit(solution)/shard_map/all_gather | solution.py:264
  58.4 0.0 copy-start.6
  58.4 1.7 %copy-done.6 = bf16[4864,256]{1,0:T(8,128)(2,1)S(1)} copy-done((bf16[4864,256]{1,0:T(8,128)(2,1)S(1)}, bf16[4864,256]{1,0:T(8,128)(2,1)}, u32[]{:S(2)}) %copy-start.6) | copy-done | bytes 2490392
  60.1 1.9 %grad.1 = (bf16[128,1152]{1,0:T(8,128)(2,1)S(1)}, bf16[1024,256]{1,0:T(8,128)(2,1)S(1)}, bf16[16,512]{1,0:T(8,128)(2,1)}) custom-call(bf16[4,1216,256]{2,1,0:T(8,128)(2,1)S(1)} %bitcast.26, bf16[4,160,256]{2,1,0:T(8,128)(2,1)S(1)} %bitcast.18, bf16[4,128,128]{2,1,0:T(8,128)(2,1)S(1)} %bitcast.24), custom_call_target="tpu_custom_call" | custom-call | flops 1048576000 | bytes 4194304 | tf_op jit(solution)/shard_map/grad/pallas_call | solution.py:296
  62.0 0.5 broadcast.14
  62.5 0.8 reduce.1
  63.3 1.1 reshape.49
  64.3 15.9 %all-to-all-start = ((bf16[128,2,576]{2,1,0:T(2,128)(2,1)}), bf16[128,2,576]{2,1,0:T(2,128)(2,1)S(1)}, u32[]{:S(2)}, u32[]{:S(2)}) async-start(bf16[128,2,576]{2,1,0:T(2,128)(2,1)} %reshape.49), calls=%async_computation | async-start | bytes 655360 | tf_op jit(solution)/shard_map/all_to_all | solution.py:307
  80.3 2.5 %collective-permute-start.2 = (bf16[128,256]{1,0:T(8,128)(2,1)S(1)}, bf16[128,256]{1,0:T(8,128)(2,1)S(1)}, u32[]{:S(2)}, u32[]{:S(2)}) collective-permute-start(bf16[128,256]{1,0:T(8,128)(2,1)S(1)} %get-tuple-element.29), channel_id=1, source_target_pairs={{0,4},{4,8},{8,12},{12,16},{16,20},{20,24},{24,28},{28,32},{32,36}... | collective-permute-start | bytes 196616 | tf_op jit(solution)/shard_map/ppermute | solution.py:305
  82.8 1.3 %collective-permute-start.3 = (bf16[128,256]{1,0:T(8,128)(2,1)S(1)}, bf16[128,256]{1,0:T(8,128)(2,1)S(1)}, u32[]{:S(2)}, u32[]{:S(2)}) collective-permute-start(bf16[128,256]{1,0:T(8,128)(2,1)S(1)} %get-tuple-element.28), channel_id=1, source_target_pairs={{4,0},{8,4},{12,8},{16,12},{20,16},{24,20},{28,24},{32,28},{36,32}... | collective-permute-start | bytes 196616 | tf_op jit(solution)/shard_map/ppermute | solution.py:306
  84.1 0.2 collective-permute-done.2.above_ref
  84.3 4.1 %collective-permute-done.3.below_ref = bf16[128,256]{1,0:T(8,128)(2,1)S(1)} collective-permute-done((bf16[128,256]{1,0:T(8,128)(2,1)S(1)}, bf16[128,256]{1,0:T(8,128)(2,1)S(1)}, u32[]{:S(2)}, u32[]{:S(2)}) %collective-permute-start.3) | collective-permute-done | bytes 65568 | tf_op jit(solution)/shard_map/ppermute | solution.py:306
  88.3 0.0 copy-start.7
  88.3 1.7 %copy-done.7 = bf16[4864,256]{1,0:T(8,128)(2,1)S(1)} copy-done((bf16[4864,256]{1,0:T(8,128)(2,1)S(1)}, bf16[4864,256]{1,0:T(8,128)(2,1)}, u32[]{:S(2)}) %copy-start.7) | copy-done | bytes 2490392
  90.0 1.6 %fine.1 = (bf16[256,256]{1,0:T(8,128)(2,1)}, bf16[256,256]{1,0:T(8,128)(2,1)}) custom-call(bf16[4,1216,256]{2,1,0:T(8,128)(2,1)S(1)} %bitcast.27, bf16[4,160,256]{2,1,0:T(8,128)(2,1)S(1)} %bitcast.19, bf16[1024,256]{1,0:T(8,128)(2,1)S(1)} %get-tuple-element.23.field_ref, bf16[128,256]{1,0:T(8,128)(2,1)S(1)} %collective-permute-done.2.above_ref, ...), custom_call_target="tpu_custom_call" | custom-call | flops 1048576000 | bytes 4194304 | tf_op jit(solution)/shard_map/fine/pallas_call | solution.py:311
  91.6 6.6 %all-to-all-done = bf16[128,2,576]{2,1,0:T(2,128)(2,1)S(1)} async-done(((bf16[128,2,576]{2,1,0:T(2,128)(2,1)}), bf16[128,2,576]{2,1,0:T(2,128)(2,1)S(1)}, u32[]{:S(2)}, u32[]{:S(2)}) %all-to-all-start) | async-done | bytes 294944 | tf_op jit(solution)/shard_map/all_to_all | solution.py:307
  98.2 0.5 reshape.50
  98.7 0.5 convert_reduce_fusion
  99.2 0.1 mul.28
  99.3 7.0 %all-gather.4 = f32[4,64,18]{1,2,0:T(8,128)S(1)} all-gather(f32[1,64,18]{1,2,0:T(8,128)S(1)} %bitcast.28), channel_id=1, replica_groups=mesh['rows'=128,'cols'=4] {'cols'}, dimensions={0}, use_global_device_ids=true | all-gather | bytes 23040 | tf_op jit(solution)/shard_map/all_gather | solution.py:310
  106.3 0.7 reshape.47
  (5 shorter events, 0.0 us)
Async XLA Ops:
  7.2 11.5 %copy-start.8 = (f32[256]{0:T(256)S(1)}, f32[256]{0:T(256)}, u32[]{:S(2)}) copy-start(f32[256]{0:T(256)} %constant.9.clone) | copy-start | bytes 3076
  7.2 11.3 %copy-start.9 = (s32[3]{0:T(128)S(1)}, s32[3]{0:T(128)}, u32[]{:S(2)}) copy-start(s32[3]{0:T(128)} %param.15) | copy-start | bytes 40
  7.2 51.2 %all-gather.7.cloned.1.call-start = ((), (), s32[]{:S(2)}) async-start(), calls=%async_computation.1 | async-start | bytes 3112960 | tf_op jit(solution)/shard_map/all_gather | solution.py:264
  8.5 24.5 %copy-start = (bf16[4608,128]{1,0:T(8,128)(2,1)S(1)}, bf16[4608,128]{1,0:T(8,128)(2,1)}, u32[]{:S(2)}) copy-start(bf16[4608,128]{1,0:T(8,128)(2,1)} %teacher_ref.3) | copy-start | bytes 3538948
  8.5 24.5 %copy-start.1 = (bf16[4608,128]{1,0:T(8,128)(2,1)S(1)}, bf16[4608,128]{1,0:T(8,128)(2,1)}, u32[]{:S(2)}) copy-start(bf16[4608,128]{1,0:T(8,128)(2,1)} %student_ref.1) | copy-start | bytes 3538948
  9.7 0.9 copy-start.3
  10.6 0.9 copy-start.4
  11.5 0.7 copy-start.5
  12.3 0.8 copy-start.2
  13.2 5.6 %collective-permute-start = (bf16[64,256]{1,0:T(8,128)(2,1)S(1)}, bf16[64,256]{1,0:T(8,128)(2,1)S(1)}, u32[]{:S(2)}, u32[]{:S(2)}) collective-permute-start(bf16[64,256]{1,0:T(8,128)(2,1)S(1)} %get-tuple-element.17), channel_id=1, source_target_pairs={{0,4},{4,8},{8,12},{12,16},{16,20},{20,24},{24,28},{28,32},{32,36}... | collective-permute-start | bytes 98312 | tf_op jit(solution)/shard_map/ppermute | solution.py:265
  17.2 4.7 %collective-permute-start.1 = (bf16[64,256]{1,0:T(8,128)(2,1)S(1)}, bf16[64,256]{1,0:T(8,128)(2,1)S(1)}, u32[]{:S(2)}, u32[]{:S(2)}) collective-permute-start(bf16[64,256]{1,0:T(8,128)(2,1)S(1)} %get-tuple-element.18), channel_id=1, source_target_pairs={{4,0},{8,4},{12,8},{16,12},{20,16},{24,20},{28,24},{32,28},{36,32}... | collective-permute-start | bytes 98312 | tf_op jit(solution)/shard_map/ppermute | solution.py:266
  58.4 1.7 %copy-start.6 = (bf16[4864,256]{1,0:T(8,128)(2,1)S(1)}, bf16[4864,256]{1,0:T(8,128)(2,1)}, u32[]{:S(2)}) copy-start(bf16[4864,256]{1,0:T(8,128)(2,1)} %all-gather.7.cloned.1.call-done) | copy-start | bytes 7471108
  64.3 33.8 %all-to-all-start = ((bf16[128,2,576]{2,1,0:T(2,128)(2,1)}), bf16[128,2,576]{2,1,0:T(2,128)(2,1)S(1)}, u32[]{:S(2)}, u32[]{:S(2)}) async-start(bf16[128,2,576]{2,1,0:T(2,128)(2,1)} %reshape.49), calls=%async_computation | async-start | bytes 655360 | tf_op jit(solution)/shard_map/all_to_all | solution.py:307
  80.3 4.0 %collective-permute-start.2 = (bf16[128,256]{1,0:T(8,128)(2,1)S(1)}, bf16[128,256]{1,0:T(8,128)(2,1)S(1)}, u32[]{:S(2)}, u32[]{:S(2)}) collective-permute-start(bf16[128,256]{1,0:T(8,128)(2,1)S(1)} %get-tuple-element.29), channel_id=1, source_target_pairs={{0,4},{4,8},{8,12},{12,16},{16,20},{20,24},{24,28},{28,32},{32,36}... | collective-permute-start | bytes 196616 | tf_op jit(solution)/shard_map/ppermute | solution.py:305
  82.8 5.6 %collective-permute-start.3 = (bf16[128,256]{1,0:T(8,128)(2,1)S(1)}, bf16[128,256]{1,0:T(8,128)(2,1)S(1)}, u32[]{:S(2)}, u32[]{:S(2)}) collective-permute-start(bf16[128,256]{1,0:T(8,128)(2,1)S(1)} %get-tuple-element.28), channel_id=1, source_target_pairs={{4,0},{8,4},{12,8},{16,12},{20,16},{24,20},{28,24},{32,28},{36,32}... | collective-permute-start | bytes 196616 | tf_op jit(solution)/shard_map/ppermute | solution.py:306
  88.3 1.7 %copy-start.7 = (bf16[4864,256]{1,0:T(8,128)(2,1)S(1)}, bf16[4864,256]{1,0:T(8,128)(2,1)}, u32[]{:S(2)}) copy-start(bf16[4864,256]{1,0:T(8,128)(2,1)} %all-gather.7.cloned.1.call-done) | copy-start | bytes 7471108
Sparse Core Ops, SparseCore 0:
  13.3 45.0 all-gather.6

commit v2 on v1

v2 whole, which is shorter than its diff:
```python
import functools
import math

import jax
import jax.numpy as jnp
from jax import lax
from jax.experimental import pallas as pl
from jax.experimental.pallas import tpu as pltpu
from jax.sharding import PartitionSpec as P

BF = jnp.bfloat16
F32 = jnp.float32
MIB = 1024 * 1024


def call(body, outs, scratch, flops, vmem, name, ins, out_spaces=None):
    out_spaces = out_spaces or [pltpu.VMEM] * len(outs)
    return pl.pallas_call(
        body,
        out_shape=outs,
        in_specs=[pl.BlockSpec(memory_space=space) for space in ins],
        out_specs=[pl.BlockSpec(memory_space=space) for space in out_spaces],
        scratch_shapes=scratch,
        compiler_params=pltpu.CompilerParams(vmem_limit_bytes=vmem * MIB),
        cost_estimate=pl.CostEstimate(flops=flops, bytes_accessed=MIB, transcendentals=0),
        name=name,
    )


def shape(dims, kind):
    return jax.ShapeDtypeStruct(dims, kind)


def silu(value):
    return value * (1.0 / (1.0 + jnp.exp(-value)))


def shifted(field, step):
    if step == 0:
        return field
    edge = jnp.zeros((field.shape[0], 1, field.shape[2]), field.dtype)
    if step < 0:
        return jnp.concatenate([edge, field[:, :-1]], axis=1)
    return jnp.concatenate([field[:, 1:], edge], axis=1)


def pack_kernel(cot_ref, mid_ref, one_ref, two_ref, sems):
    even = lax.axis_index("rows") % 2 == 0
    last, first = pl.multiple_of(jnp.where(even, 224, 0), 32), pl.multiple_of(jnp.where(even, 0, 224), 32)
    moves = [
        (mid_ref.at[:, 256 * half : 256 * half + 256], ref.at[16 * half : 16 * half + 16, :])
        for ref in (one_ref, two_ref)
        for half in range(2)
    ]
    moves += [
        (cot_ref.at[pl.ds(last, 32), :], one_ref.at[32:64, :]),
        (cot_ref.at[pl.ds(first, 32), :], two_ref.at[32:64, :]),
    ]
    for copy in start_all(moves, sems):
        copy.wait()


def near_at(row):
    even = row % 2 == 0
    above = pl.multiple_of(jnp.where(even, 128, 0), 64)
    below = pl.multiple_of(jnp.where(even, 64, 128), 64)
    return above, below, pl.multiple_of(jnp.where(even, 0, 64), 64)


def start_all(moves, sems):
    copies = [pltpu.make_async_copy(src, dst, sems.at[n]) for n, (src, dst) in enumerate(moves)]
    for copy in copies:
        copy.start()
    return copies


def waves(angle):
    turns = jnp.round(angle * (0.5 / math.pi))
    rest = (angle - turns * 6.28125) - turns * (2 * math.pi - 6.28125)
    square = rest * rest
    sin, cos = jnp.ones_like(rest), jnp.ones_like(rest)
    for n in range(9, 0, -1):
        cos = 1.0 - square * cos * (1.0 / ((2 * n - 1) * (2 * n)))
        sin = 1.0 - square * sin * (1.0 / ((2 * n) * (2 * n + 1)))
    return rest * sin, cos


def embed(step):
    index = lax.broadcasted_iota(jnp.int32, (1, 256), 1)
    freqs = jnp.ones((1, 256), F32)
    for bit in range(8):
        factor = math.exp(-math.log(10000.0) * 2**bit / 256)
        freqs = jnp.where((index // 2**bit) % 2 == 1, freqs * factor, freqs)
    return jnp.concatenate(waves(step.astype(F32) * freqs), axis=1)


def delta(steps_ref, n):
    return (steps_ref[:, n + 1 : n + 2] - steps_ref[:, n : n + 1]).astype(F32) / 1000.0


def first_kernel(
    near_ref, teacher_ref, pupil_ref, steps_ref, cot_ref, proj_ref,
    sec_ref, mid_ref, base_ref,
    tile_ref, raw_ref, wave_ref, in_ref, sems,
):
    row, col = lax.axis_index("rows"), lax.axis_index("cols")
    last = lax.axis_size("rows") - 1
    above, below, own = near_at(row)
    moves = [(near_ref.at[:, pl.ds(start, 32), :], tile_ref.at[n]) for n, start in enumerate((above, own, below))]
    moves += [
        (cot_ref.at[:, 128 * n : 128 * n + 128], sec_ref.at[128 + 256 * n : 384 + 256 * n, :]) for n in range(2)
    ]
    moves += [
        (proj_ref.at[:, 128 * n : 128 * n + 128], sec_ref.at[640 + 64 * n : 704 + 64 * n, :]) for n in range(4)
    ]
    copies = start_all(moves, sems)
    for n in range(2):
        wave_ref[n : n + 1, :] = embed(steps_ref[:, n : n + 1])
    lines = []
    for n in range(3):
        copies[n].wait()
        tiles = [tile_ref[n, s].astype(F32) for s in range(4)]
        for half in (0, 8):
            lines.append(
                jnp.concatenate(
                    [jnp.concatenate([t[half : half + 8], t[half + 16 : half + 24]], axis=1) for t in tiles],
                    axis=0,
                )
            )
    raw = jnp.stack(lines)
    raw_ref[...] = raw.reshape(192, 512)
    lit = silu(raw + wave_ref[0:1, :].reshape(1, 1, 512))
    line = lax.broadcasted_iota(jnp.int32, (6, 32, 512), 0)
    inside = ((line >= 2) | (row > 0)) & ((line < 4) | (row < last))
    lit = jnp.where(inside, lit, 0.0)
    for at, step in enumerate((-1, 0, 1)):
        in_ref[at] = shifted(lit, step).astype(BF).reshape(192, 512)
    total = jnp.zeros((128, 128), F32)
    for dy in range(3):
        for dx in range(3):
            k = (3 * dy + dx) * 512
            total += jnp.dot(
                in_ref[dx, 32 * dy : 32 * dy + 128, :], teacher_ref[k : k + 512, :], preferred_element_type=F32
            )
    own = pl.ds(pl.multiple_of(col * 128, 128), 128)
    anchor = raw_ref[32:160, own]
    one, two = delta(steps_ref, 0), delta(steps_ref, 1)
    middle = anchor + one * total
    second = silu(middle + wave_ref[1:2, own])
    line = lax.broadcasted_iota(jnp.int32, (128, 128), 0)
    inside = ((line >= 32) | (row > 0)) & ((line < 96) | (row < last))
    sec_ref[0:128, :] = jnp.where(inside, second, 0.0).astype(BF)
    mid_ref[...] = middle[32:96]
    total = jnp.zeros((64, 128), F32)
    for dy in range(3):
        for dx in range(3):
            k = (3 * dy + dx) * 512
            total += jnp.dot(
                in_ref[dx, 32 * dy + 32 : 32 * dy + 96, :], pupil_ref[k : k + 512, :], preferred_element_type=F32
            )
    base_ref[...] = anchor[32:96] + (one + two) * total
    for copy in copies[3:]:
        copy.wait()


def weight_moves(turned_ref, first, out_ref, base):
    return [
        (turned_ref.at[:, 128 * (first + n) : 128 * (first + n) + 128], out_ref.at[base + 64 * n : base + 64 * n + 64, :])
        for n in range(9)
    ]


def second_kernel(sec_ref, teacher_ref, mid_ref, base_ref, steps_ref, turned_ref, out_ref, in_ref, sems):
    copies = start_all(weight_moves(turned_ref, 0, out_ref, 128), sems)
    field = jnp.concatenate([sec_ref[s, 0:128, :] for s in range(4)], axis=1).astype(F32).reshape(4, 32, 512)
    for at, step in enumerate((-1, 0, 1)):
        in_ref[at] = shifted(field, step).astype(BF).reshape(128, 512)
    total = jnp.zeros((64, 128), F32)
    for dy in range(3):
        for dx in range(3):
            k = (3 * dy + dx) * 512
            total += jnp.dot(
                in_ref[dx, 32 * dy : 32 * dy + 64, :], teacher_ref[k : k + 512, :], preferred_element_type=F32
            )
    target = mid_ref[...] + delta(steps_ref, 1) * total
    out_ref[0:64, :] = target.astype(BF)
    out_ref[64:128, :] = (target - base_ref[...]).astype(BF)
    for copy in copies:
        copy.wait()


def repeater():
    place = lax.broadcasted_iota(jnp.int32, (128, 32), 0) // 4
    return (place == lax.broadcasted_iota(jnp.int32, (128, 32), 1)).astype(BF)


def lifted(target, proj):
    wide = jnp.dot(repeater(), target, preferred_element_type=F32).astype(BF)
    return lax.dot_general(wide, proj, (((1,), (1,)), ((), ())), preferred_element_type=F32)


def grad_kernel(
    near_ref, sec_ref, late_ref, part_ref, field_ref, one_ref, two_ref, gap_ref, line_ref, sum_ref, gap_scratch
):
    row, col = lax.axis_index("rows"), lax.axis_index("cols")
    above, below, _ = near_at(row)
    even = row % 2 == 0
    pair = pl.multiple_of((col // 2) * 128, 128)
    lanes = pl.ds(pair, 128)
    target = jnp.concatenate([late_ref[s, 0:64, :] for s in range(4)], axis=1)
    proj = jnp.concatenate(
        [
            jnp.concatenate([sec_ref[s, 640 + 64 * n : 704 + 64 * n, :] for n in range(4)], axis=1)
            for s in range(4)
        ],
        axis=0,
    )
    for m in range(2):
        lift = lifted(target[32 * m : 32 * m + 32], proj)
        for i in range(4 * m, 4 * m + 4):
            noisy = jnp.concatenate([near_ref[s, 192 + 32 * i : 224 + 32 * i, :] for s in range(4)], axis=0)
            line_ref[128 * i : 128 * i + 128, :] = (noisy.astype(F32) + lift).astype(BF)
    begin = pl.multiple_of(32 * col, 32)
    before = pl.multiple_of(jnp.maximum(32 * col - 16, 0), 16)
    after = pl.multiple_of(jnp.minimum(32 * col + 32, 112), 16)
    for i in range(8):
        for at, to, size in ((before, 0, 16), (begin, 16, 32), (after, 48, 16)):
            field_ref[i, to : to + size, :] = line_ref[pl.ds(128 * i + at, size), :]
    one_ref[...] = jnp.where(even, line_ref[896:1024, :], line_ref[0:128, :])
    two_ref[...] = jnp.where(even, line_ref[0:128, :], line_ref[896:1024, :])
    gap_scratch[...] = jnp.concatenate([late_ref[s, 64:128, :] for s in range(4)], axis=1).astype(F32)
    gap_ref[...] = jnp.concatenate(
        [gap_scratch[pl.ds(pl.multiple_of(32 * i + 8 * col, 8), 8), :] for i in range(2)], axis=0
    ).astype(BF)
    lines = [near_ref[s, pl.ds(above + 32, 32), lanes] for s in range(4)]
    for i in range(8):
        lines += [sec_ref[s, pl.ds(128 + 32 * i + 2 * pair, 32), :] for s in range(4)]
    lines += [near_ref[s, pl.ds(below + 32, 32), lanes] for s in range(4)]
    cot = jnp.concatenate(lines, axis=0).astype(F32)
    cot = jnp.where(col % 2 == 1, cot[:, 64:128], cot[:, 0:64]).reshape(10, 128, 64)
    moved = jnp.concatenate([shifted(cot, -dx) for dx in (-1, 0, 1)], axis=2).astype(BF).reshape(1280, 192)
    field = line_ref[...]
    for dy in (-1, 0, 1):
        term = lax.dot_general(
            field,
            moved[(1 - dy) * 128 : (1 - dy) * 128 + 1024],
            (((0,), (0,)), ((), ())),
            preferred_element_type=F32,
        )
        for dx in range(3):
            one = term[:, 64 * dx : 64 * dx + 64]
            at = (3 * (dy + 1) + dx) * 256
            sum_ref[at : at + 256, :] = jnp.concatenate([one, one], axis=1)
    owners = part_ref.shape[0]
    each = 2304 // owners
    lane = lax.broadcasted_iota(jnp.int32, (owners, 128), 1)

    def line(j):
        if 2 * j >= each:
            return jnp.zeros((owners, 128), F32)
        even_line = sum_ref[pl.ds(2 * j, owners, stride=each), :]
        odd_line = sum_ref[pl.ds(2 * j + 1, owners, stride=each), :]
        return jnp.where(lane < 64, even_line, odd_line)

    for j in range(5):
        part_ref[:, :, 128 * j : 128 * j + 128] = jnp.stack([line(j), line(j + 5)], axis=1).astype(BF)
def share_kernel(scale, part_ref, turned_ref, share_ref, sems):
    copies = start_all(weight_moves(turned_ref, 9, share_ref, 32), sems)
    total = jnp.sum(part_ref[...].astype(F32), axis=0) * scale
    rows = []
    for j in range(9):
        line = total[j // 5 : j // 5 + 1, 128 * (j % 5) : 128 * (j % 5) + 128]
        rows += [line[:, 0:64], line[:, 64:128]]
    own = jnp.concatenate(rows + [jnp.zeros((14, 64), F32)], axis=0)
    high = own.astype(BF).astype(F32)
    share_ref[0:32, :] = jnp.concatenate([high, own - high], axis=1).astype(BF)
    for copy in copies:
        copy.wait()


def fine_kernel(
    near_ref, sec_ref, late_ref, share_ref, field_ref, one_ref, two_ref,
    out_ref, back_ref, grad_ref,
    weight_ref, tile_ref, in_ref,
):
    row, col = lax.axis_index("rows"), lax.axis_index("cols")
    even = row % 2 == 0
    above, below, _ = near_at(row)
    owned = [share_ref[s, 0:32, :].astype(F32) for s in range(4)]
    grad_ref[...] = jnp.concatenate([(own[:, 0:64] + own[:, 64:128])[0:18] for own in owned], axis=1)
    for s in range(4):
        for n in range(9):
            weight_ref[64 * s : 64 * s + 64, 128 * n : 128 * n + 128] = late_ref[s, 128 + 64 * n : 192 + 64 * n, :]
            weight_ref[64 * s : 64 * s + 64, 1152 + 128 * n : 1280 + 128 * n] = share_ref[
                s, 32 + 64 * n : 96 + 64 * n, :
            ]
    place = lax.broadcasted_iota(jnp.int32, (10, 64, 256), 1)
    framed = ((place >= 16) | (col > 0)) & ((place < 48) | (col < 3))

    def lay_out():
        wide = jnp.where(framed, tile_ref[...].astype(F32), 0.0)
        for at in range(3):
            in_ref[at] = wide[:, 15 + at : 47 + at].astype(BF).reshape(320, 256)

    begin = pl.multiple_of(32 * col, 32)
    before = pl.multiple_of(jnp.maximum(32 * col - 16, 0), 16)
    after = pl.multiple_of(jnp.minimum(32 * col + 32, 112), 16)
    for at, to, size in ((before, 0, 16), (begin, 16, 32), (after, 48, 16)):
        one, two = one_ref[pl.ds(at, size), :], two_ref[pl.ds(at, size), :]
        tile_ref[0, to : to + size, :] = jnp.where(even, two, one)
        tile_ref[9, to : to + size, :] = jnp.where(even, one, two)
    tile_ref[1:9] = field_ref[...]
    lay_out()
    total = jnp.zeros((256, 256), F32)
    for dy in range(3):
        for dx in range(3):
            k = (3 * dy + dx) * 256
            total += lax.dot_general(
                in_ref[dx, 32 * dy : 32 * dy + 256, :],
                weight_ref[:, k : k + 256],
                (((1,), (1,)), ((), ())),
                preferred_element_type=F32,
            )
    out_ref[...] = total.astype(BF)

    left, right = jnp.maximum(col - 1, 0), jnp.minimum(col + 1, 3)
    for tile, at, to, size in ((left, 16, 0, 16), (col, 0, 16, 32), (right, 0, 48, 16)):
        for i, start in ((0, above), (9, below)):
            tile_ref[i, to : to + size, :] = near_ref[tile, pl.ds(start + 32 + at, size), :]
        for i in range(8):
            for half in range(2):
                first = 128 + 256 * half + 32 * i + at
                tile_ref[i + 1, to : to + size, 128 * half : 128 * half + 128] = sec_ref[tile, first : first + size, :]
    lay_out()
    total = jnp.zeros((256, 256), F32)
    for dy in range(3):
        for dx in range(3):
            k = (3 * dy + dx) * 256
            total += jnp.dot(
                in_ref[2 - dx, 32 * (2 - dy) : 32 * (2 - dy) + 256, :],
                weight_ref[:, k : k + 256],
                preferred_element_type=F32,
            )
    back_ref[...] = total.astype(BF)


def on_device(
    fine_noisy, fine_weight, projection, mid_noisy, teacher_weight, student_weight, steps, cotangent
):
    count = lax.axis_size("rows")
    near_pairs = [(i ^ 1, i) for i in range(count)]
    far_pairs = [(i, i + 1 if i % 2 else i - 1) for i in range(1, count - 1)]

    turned = fine_weight.T
    flat = cotangent.reshape(256, 256)
    one, two = call(
        pack_kernel,
        [shape((64, 256), BF), shape((64, 256), BF)],
        [pltpu.SemaphoreType.DMA((6,))],
        MIB,
        56,
        "pack",
        [pl.ANY] * 2,
    )(flat, mid_noisy.reshape(16, 512))
    two = lax.ppermute(two, "rows", far_pairs)
    pairs = [[i, i + 1] for i in range(0, count, 2)]
    one = lax.all_gather(one, "rows", axis=0, tiled=True, axis_index_groups=pairs)
    near = lax.all_gather(jnp.concatenate([one, two, fine_noisy.reshape(256, 256)], axis=0), "cols", axis=0)
    steps = steps.reshape(1, 3)
    sec, middle, base = call(
        first_kernel,
        [shape((896, 128), BF), shape((64, 128), F32), shape((64, 128), F32)],
        [
            pltpu.VMEM((3, 4, 32, 256), BF),
            pltpu.VMEM((192, 512), F32),
            pltpu.VMEM((2, 512), F32),
            pltpu.VMEM((3, 192, 512), BF),
            pltpu.SemaphoreType.DMA((9,)),
        ],
        300 * MIB,
        16,
        "first",
        [pl.ANY] + [pltpu.VMEM] * 3 + [pl.ANY] * 2,
    )(near, teacher_weight, student_weight, steps, flat, projection.T)
    sec = lax.all_gather(sec, "cols", axis=0)
    (late,) = call(
        second_kernel,
        [shape((704, 128), BF)],
        [pltpu.VMEM((3, 128, 512), BF), pltpu.SemaphoreType.DMA((9,))],
        100 * MIB,
        16,
        "second",
        [pltpu.VMEM] * 5 + [pl.ANY],
    )(sec, teacher_weight, middle, base, steps, turned)
    late = lax.all_gather(late, "cols", axis=0)
    part, field, one, two, gap = call(
        grad_kernel,
        [
            shape((count, 2, 640), BF),
            shape((8, 64, 256), BF),
            shape((128, 256), BF),
            shape((128, 256), BF),
            shape((16, 512), BF),
        ],
        [pltpu.VMEM((1024, 256), BF), pltpu.VMEM((2304, 128), F32), pltpu.VMEM((64, 512), F32)],
        1000 * MIB,
        32,
        "grad",
        [pltpu.VMEM] * 3,
    )(near, sec, late)
    part = lax.all_to_all(part, "rows", 0, 0, tiled=True)
    two = lax.ppermute(two, "rows", far_pairs)
    one = lax.ppermute(one, "rows", near_pairs)
    (share,) = call(
        functools.partial(share_kernel, 1.0 / math.sqrt(1024 * count)),
        [shape((608, 128), BF)],
        [pltpu.SemaphoreType.DMA((9,))],
        MIB,
        8,
        "share",
        [pltpu.VMEM, pl.ANY],
    )(part, turned)
    share = lax.all_gather(share, "cols", axis=0)
    share, one, two = lax.optimization_barrier((share, one, two))
    fine_out, grad_input, grad_weight = call(
        fine_kernel,
        [shape((256, 256), BF), shape((256, 256), BF), shape((18, 256), F32)],
        [pltpu.VMEM((256, 2304), BF), pltpu.VMEM((10, 64, 256), BF), pltpu.VMEM((3, 320, 256), BF)],
        1000 * MIB,
        32,
        "fine",
        [pltpu.VMEM] * 7,
    )(near, sec, late, share, field, one, two)
    return (
        fine_out.reshape(8, 32, 256),
        grad_input.reshape(8, 32, 256),
        grad_weight,
        gap.reshape(2, 8, 512),
    )


def solution(mesh):
    placed = (
        P("rows", "cols", None),
        P(None, "cols"),
        P(None, "cols"),
        P("rows", "cols", None),
        P(None, "cols"),
        P(None, "cols"),
        P(),
        P("rows", "cols", None),
    )
    return jax.shard_map(
        on_device,
        mesh=mesh,
        in_specs=placed,
        out_specs=(
            P("rows", "cols", None),
            P("rows", "cols", None),
            P("rows", None),
            P("rows", "cols", None),
        ),
        check_vma=False,
    )
```

time: 114 us -> 97.9 us (0.86)
  blocking collectives: 30.2 us -> 46.8 us
  between operations: 14.2 us -> 0.77 us
  waiting for transfers between devices: 26.3 us -> 14.5 us
  local copies, waits for them, and re-layouts: 12.1 us -> 1.99 us
  Pallas kernels: 4.44 us -> 7.79 us
    all_gather x1 -> x0, waiting for transfers between devices: 12.5 us -> none  [on_device(): bulk = lax.all_gather(bulk, 'cols', axis=0)]
    all_gather x2 -> x3, blocking collectives: 18.2 us -> 28.8 us  [the longest x1 13.1 us: on_device(): lax.all_gather(jnp.concatenate([one, two, fine_noisy.reshape(256, 256)],...]
    unnamed x25 -> x16, local copies, waits for them, and re-layouts: 11.4 us -> 1.99 us
    all_to_all x1, waiting for transfers between devices: 6.55 us -> 14.5 us  [on_device(): part = lax.all_to_all(part, 'rows', 0, 0, tiled=True)]
    ppermute x4 -> x3, waiting for transfers between devices: 7.27 us -> 0.01 us  [the longest x2 0.01 us: on_device(): two = lax.ppermute(two, 'rows', far_pairs)]
    ppermute x4 -> x3, starting transfers between devices: 9.03 us -> 3.81 us  [the longest x1 2.48 us: on_device(): one = lax.ppermute(one, 'rows', near_pairs)]
    all_to_all x1, starting transfers between devices: 15.9 us -> 21 us  [on_device(): part = lax.all_to_all(part, 'rows', 0, 0, tiled=True)]
    all_gather x1, blocking collectives: 5.82 us -> 9.57 us  [on_device(): sec = lax.all_gather(sec, 'cols', axis=0)]
  transfers between devices with their start and end apart: 6 -> 4, of which waited for: 5 -> 1; matrix products, arithmetic and copies ran while one was open for 0% -> 0% of each run, Pallas kernels for 2% -> 1%
where the time goes in v2:
time: 97.9 us; the launch traced here: 97.5 us
  blocking collectives  46.8 us (48%)
  starting transfers between devices  24.8 us (25%)
  waiting for transfers between devices  14.5 us (15%)
  Pallas kernels  7.79 us (8%)
  local copies, waits for them, and re-layouts  1.99 us (2%)
    all_to_all x1, starting transfers between devices, on_device(): part = lax.all_to_all(part, 'rows', 0, 0, tiled=True)  21 us
    all_to_all x1, waiting for transfers between devices, on_device(): part = lax.all_to_all(part, 'rows', 0, 0, tiled=True)  14.5 us
    all_gather x1, blocking collectives, on_device(): lax.all_gather(jnp.concatenate([one, two, fine_noisy.reshape(256, 256)],...  13.1 us
    all_gather x1, blocking collectives, on_device(): sec = lax.all_gather(sec, 'cols', axis=0)  9.57 us
    all_gather x1, blocking collectives, on_device(): share = lax.all_gather(share, 'cols', axis=0)  9.01 us
    all_gather x1, blocking collectives, on_device(): late = lax.all_gather(late, 'cols', axis=0)  8.36 us
    all_gather x1, blocking collectives, on_device(): lax.all_gather(one, 'rows', axis=0, tiled=True, axis_index_groups=pairs)  6.73 us
    pallas_call x1, Pallas kernels, on_device(): call(grad_kernel, [shape((count, 2, 640), BF), shape((8, 64, 256), BF), s...  2.59 us
  transfers between devices with their start and end apart: 4, of which 1 were waited for; matrix products, arithmetic and copies ran while one was open for 0% of the time, Pallas kernels for 1%

profile of v2, /device:TPU:1, one launch (start us, length us, event | category | flops | bytes accessed | tf_op | source)
XLA Modules:
  0.0 97.5 jit_solution(2932651872315890829)
XLA Ops:
  0.6 0.0 copy-start.3
  0.6 0.0 copy-start
  0.7 0.0 copy-start.5
  0.7 0.0 copy-start.4
  0.7 1.6 %pack.1 = (bf16[64,256]{1,0:T(8,128)(2,1)}, bf16[64,256]{1,0:T(8,128)(2,1)}) custom-call(bf16[256,256]{1,0:T(8,128)(2,1)} %bitcast.24, bf16[16,512]{1,0:T(8,128)(2,1)} %bitcast.30), custom_call_target="tpu_custom_call" | custom-call | flops 1048576 | bytes 1048576 | tf_op jit(solution)/shard_map/pack/pallas_call | solution.py:356
  2.2 0.7 collective-permute-start
  2.9 6.7 %all_gather.27 = bf16[128,256]{1,0:T(8,128)(2,1)S(1)} all-gather(bf16[64,256]{1,0:T(8,128)(2,1)} %get-tuple-element.20), channel_id=1, replica_groups={{0,4},{8,12},{16,20},{24,28},{32,36},{40,44},{48,52},{56,60},{64,68},{7..., dimensions={0}, use_global_device_ids=true | all-gather | bytes 98304 | tf_op jit(solution)/shard_map/all_gather | solution.py:367
  9.7 0.0 collective-permute-done
  9.7 0.9 pad_maximum_fusion
  10.6 13.1 %all-gather = bf16[1792,256]{1,0:T(8,128)(2,1)S(1)} all-gather(bf16[448,256]{1,0:T(8,128)(2,1)S(1)} %pad_maximum_fusion), channel_id=2, replica_groups=mesh['rows'=128,'cols'=4] {'cols'}, dimensions={0}, use_global_device_ids=true | all-gather | bytes 1146880 | tf_op jit(solution)/shard_map/all_gather | solution.py:368
  23.7 0.0 copy-done.3
  23.7 0.0 copy-done
  23.7 0.0 copy-done.5
  23.7 0.0 copy-done.4
  23.7 0.0 copy-start.1
  23.7 1.3 %copy-done.1 = bf16[4608,128]{1,0:T(8,128)(2,1)S(1)} copy-done((bf16[4608,128]{1,0:T(8,128)(2,1)S(1)}, bf16[4608,128]{1,0:T(8,128)(2,1)}, u32[]{:S(2)}) %copy-start.1) | copy-done | bytes 1179672
  25.0 1.0 %first.1 = (bf16[896,128]{1,0:T(8,128)(2,1)S(1)}, f32[64,128]{1,0:T(8,128)S(1)}, f32[64,128]{1,0:T(8,128)S(1)}) custom-call(bf16[4,448,256]{2,1,0:T(8,128)(2,1)S(1)} %bitcast.13, bf16[4608,128]{1,0:T(8,128)(2,1)S(1)} %copy-done, bf16[4608,128]{1,0:T(8,128)(2,1)S(1)} %copy-done.1, s32[1,3]{1,0:T(1,128)S(1)} %bitcast.27, bf16[256,256]{1,0:T(8,128)(2,1)S(1)} %bitcast.25, ...), custom_call_target="tpu_custom_call" | custom-call | flops 314572800 | bytes 1048576 | tf_op jit(solution)/shard_map/first/pallas_call | solution.py:370
  25.9 0.0 copy-start.2
  26.0 9.6 %all-gather.1 = bf16[3584,128]{1,0:T(8,128)(2,1)S(1)} all-gather(bf16[896,128]{1,0:T(8,128)(2,1)S(1)} %get-tuple-element.22), channel_id=3, replica_groups=mesh['rows'=128,'cols'=4] {'cols'}, dimensions={0}, use_global_device_ids=true | all-gather | bytes 1146880 | tf_op jit(solution)/shard_map/all_gather | solution.py:385
  35.5 0.0 copy-done.2
  35.5 0.5 second.1
  36.0 8.4 %all-gather.2 = bf16[2816,128]{1,0:T(8,128)(2,1)S(1)} all-gather(bf16[704,128]{1,0:T(8,128)(2,1)S(1)} %second.1), channel_id=4, replica_groups=mesh['rows'=128,'cols'=4] {'cols'}, dimensions={0}, use_global_device_ids=true | all-gather | bytes 901120 | tf_op jit(solution)/shard_map/all_gather | solution.py:395
  44.4 2.6 %grad.1 = (bf16[128,2,640]{2,1,0:T(2,128)(2,1)}, bf16[8,64,256]{2,1,0:T(8,128)(2,1)S(1)}, bf16[128,256]{1,0:T(8,128)(2,1)S(1)}, bf16[128,256]{1,0:T(8,128)(2,1)S(1)}, bf16[16,512]{1,0:T(8,128)(2,1)}) custom-call(bf16[4,448,256]{2,1,0:T(8,128)(2,1)S(1)} %bitcast.14, bf16[4,896,128]{2,1,0:T(8,128)(2,1)S(1)} %bitcast.17, bf16[4,704,128]{2,1,0:T(8,128)(2,1)S(1)} %bitcast.21), custom_call_target="tpu_custom_call" | custom-call | flops 1048576000 | bytes 1048576 | tf_op jit(solution)/shard_map/grad/pallas_call | solution.py:396
  47.0 0.0 copy-start.6
  47.0 0.7 copy-done.6
  47.6 21.0 %all-to-all-start = ((bf16[128,2,640]{2,1,0:T(2,128)(2,1)}), bf16[128,2,640]{2,1,0:T(2,128)(2,1)S(1)}, u32[]{:S(2)}, u32[]{:S(2)}) async-start(bf16[128,2,640]{2,1,0:T(2,128)(2,1)} %get-tuple-element.25), calls=%async_computation | async-start | bytes 655360 | tf_op jit(solution)/shard_map/all_to_all | solution.py:411
  68.6 2.5 %collective-permute-start.1 = (bf16[128,256]{1,0:T(8,128)(2,1)S(1)}, bf16[128,256]{1,0:T(8,128)(2,1)S(1)}, u32[]{:S(2)}, u32[]{:S(2)}) collective-permute-start(bf16[128,256]{1,0:T(8,128)(2,1)S(1)} %get-tuple-element.26), channel_id=1, source_target_pairs={{4,0},{0,4},{12,8},{8,12},{20,16},{16,20},{28,24},{24,28},{36,32},... | collective-permute-start | bytes 196616 | tf_op jit(solution)/shard_map/ppermute | solution.py:413
  71.1 0.7 collective-permute-start.2
  71.8 14.5 %all-to-all-done.part_ref = bf16[128,2,640]{2,1,0:T(2,128)(2,1)S(1)} async-done(((bf16[128,2,640]{2,1,0:T(2,128)(2,1)}), bf16[128,2,640]{2,1,0:T(2,128)(2,1)S(1)}, u32[]{:S(2)}, u32[]{:S(2)}) %all-to-all-start) | async-done | bytes 327712 | tf_op jit(solution)/shard_map/all_to_all | solution.py:411
  86.3 0.0 copy-start.7
  86.3 0.6 share.1
  86.9 9.0 %all-gather.3 = bf16[2432,128]{1,0:T(8,128)(2,1)S(1)} all-gather(bf16[608,128]{1,0:T(8,128)(2,1)S(1)} %share.1), channel_id=5, replica_groups=mesh['rows'=128,'cols'=4] {'cols'}, dimensions={0}, use_global_device_ids=true | all-gather | bytes 778240 | tf_op jit(solution)/shard_map/all_gather | solution.py:423
  96.0 0.0 collective-permute-done.1.one_ref
  96.0 0.0 collective-permute-done.2.two_ref
  96.0 0.0 copy-done.7
  96.0 1.6 %fine.1 = (bf16[256,256]{1,0:T(8,128)(2,1)}, bf16[256,256]{1,0:T(8,128)(2,1)}, f32[18,256]{1,0:T(8,128)}) custom-call(bf16[4,448,256]{2,1,0:T(8,128)(2,1)S(1)} %bitcast.15, bf16[4,896,128]{2,1,0:T(8,128)(2,1)S(1)} %bitcast.18, bf16[4,704,128]{2,1,0:T(8,128)(2,1)S(1)} %bitcast.22, bf16[4,608,128]{2,1,0:T(8,128)(2,1)S(1)} %bitcast.23, ...), custom_call_target="tpu_custom_call" | custom-call | flops 1048576000 | bytes 1048576 | tf_op jit(solution)/shard_map/fine/pallas_call | solution.py:425
Async XLA Ops:
  0.6 23.0 %copy-start.3 = (bf16[8,32,256]{2,1,0:T(8,128)(2,1)S(1)}, bf16[8,32,256]{2,1,0:T(8,128)(2,1)}, u32[]{:S(2)}) copy-start(bf16[8,32,256]{2,1,0:T(8,128)(2,1)} %param.15) | copy-start | bytes 393220
  0.6 23.0 %copy-start = (bf16[4608,128]{1,0:T(8,128)(2,1)S(1)}, bf16[4608,128]{1,0:T(8,128)(2,1)}, u32[]{:S(2)}) copy-start(bf16[4608,128]{1,0:T(8,128)(2,1)} %teacher_ref.3) | copy-start | bytes 3538948
  0.7 23.0 %copy-start.5 = (s32[3]{0:T(128)S(1)}, s32[3]{0:T(128)}, u32[]{:S(2)}) copy-start(s32[3]{0:T(128)} %param.14) | copy-start | bytes 40
  0.7 23.0 %copy-start.4 = (bf16[512,64]{0,1:T(8,128)(2,1)S(1)}, bf16[512,64]{0,1:T(8,128)(2,1)}, u32[]{:S(2)}) copy-start(bf16[512,64]{0,1:T(8,128)(2,1)} %param.10) | copy-start | bytes 196612
  2.2 7.4 %collective-permute-start = (bf16[64,256]{1,0:T(8,128)(2,1)}, bf16[64,256]{1,0:T(8,128)(2,1)S(1)}, u32[]{:S(2)}, u32[]{:S(2)}) collective-permute-start(bf16[64,256]{1,0:T(8,128)(2,1)} %get-tuple-element.21), channel_id=1, source_target_pairs={{4,8},{8,4},{12,16},{16,12},{20,24},{24,20},{28,32},{32,28},{36,40... | collective-permute-start | bytes 98312 | tf_op jit(solution)/shard_map/ppermute | solution.py:365
  23.7 1.3 %copy-start.1 = (bf16[4608,128]{1,0:T(8,128)(2,1)S(1)}, bf16[4608,128]{1,0:T(8,128)(2,1)}, u32[]{:S(2)}) copy-start(bf16[4608,128]{1,0:T(8,128)(2,1)} %pupil_ref.1) | copy-start | bytes 3538948
  25.9 9.6 %copy-start.2 = (bf16[2304,64]{0,1:T(8,128)(2,1)S(1)}, bf16[2304,64]{0,1:T(8,128)(2,1)}, u32[]{:S(2)}) copy-start(bf16[2304,64]{0,1:T(8,128)(2,1)} %param.9) | copy-start | bytes 884740
  47.0 0.7 copy-start.6
  47.6 38.7 %all-to-all-start = ((bf16[128,2,640]{2,1,0:T(2,128)(2,1)}), bf16[128,2,640]{2,1,0:T(2,128)(2,1)S(1)}, u32[]{:S(2)}, u32[]{:S(2)}) async-start(bf16[128,2,640]{2,1,0:T(2,128)(2,1)} %get-tuple-element.25), calls=%async_computation | async-start | bytes 655360 | tf_op jit(solution)/shard_map/all_to_all | solution.py:411
  68.6 27.3 %collective-permute-start.1 = (bf16[128,256]{1,0:T(8,128)(2,1)S(1)}, bf16[128,256]{1,0:T(8,128)(2,1)S(1)}, u32[]{:S(2)}, u32[]{:S(2)}) collective-permute-start(bf16[128,256]{1,0:T(8,128)(2,1)S(1)} %get-tuple-element.26), channel_id=1, source_target_pairs={{4,0},{0,4},{12,8},{8,12},{20,16},{16,20},{28,24},{24,28},{36,32},... | collective-permute-start | bytes 196616 | tf_op jit(solution)/shard_map/ppermute | solution.py:413
  71.1 24.8 %collective-permute-start.2 = (bf16[128,256]{1,0:T(8,128)(2,1)S(1)}, bf16[128,256]{1,0:T(8,128)(2,1)S(1)}, u32[]{:S(2)}, u32[]{:S(2)}) collective-permute-start(bf16[128,256]{1,0:T(8,128)(2,1)S(1)} %get-tuple-element.27), channel_id=1, source_target_pairs={{4,8},{8,4},{12,16},{16,12},{20,24},{24,20},{28,32},{32,28},{36,40... | collective-permute-start | bytes 196616 | tf_op jit(solution)/shard_map/ppermute | solution.py:412
  86.3 9.7 %copy-start.7 = (bf16[8,64,256]{2,1,0:T(8,128)(2,1)S(1)}, bf16[8,64,256]{2,1,0:T(8,128)(2,1)}, u32[]{:S(2)}) copy-start(bf16[8,64,256]{2,1,0:T(8,128)(2,1)} %copy-done.6) | copy-start | bytes 786436

commit v3 on v2

--- a/solution.py
+++ b/solution.py
@@ -99,8 +99,8 @@
 
 
 def first_kernel(
-    near_ref, teacher_ref, pupil_ref, steps_ref, cot_ref, proj_ref,
-    sec_ref, mid_ref, base_ref,
+    near_ref, teacher_ref, steps_ref, cot_ref, proj_ref,
+    sec_ref, mid_ref, anchor_ref, lit_ref,
     tile_ref, raw_ref, wave_ref, in_ref, sems,
 ):
     row, col = lax.axis_index("rows"), lax.axis_index("cols")
@@ -144,34 +144,35 @@
             )
     own = pl.ds(pl.multiple_of(col * 128, 128), 128)
     anchor = raw_ref[32:160, own]
-    one, two = delta(steps_ref, 0), delta(steps_ref, 1)
-    middle = anchor + one * total
+    middle = anchor + delta(steps_ref, 0) * total
     second = silu(middle + wave_ref[1:2, own])
     line = lax.broadcasted_iota(jnp.int32, (128, 128), 0)
     inside = ((line >= 32) | (row > 0)) & ((line < 96) | (row < last))
     sec_ref[0:128, :] = jnp.where(inside, second, 0.0).astype(BF)
     mid_ref[...] = middle[32:96]
-    total = jnp.zeros((64, 128), F32)
-    for dy in range(3):
-        for dx in range(3):
-            k = (3 * dy + dx) * 512
-            total += jnp.dot(
-                in_ref[dx, 32 * dy + 32 : 32 * dy + 96, :], pupil_ref[k : k + 512, :], preferred_element_type=F32
-            )
-    base_ref[...] = anchor[32:96] + (one + two) * total
+    anchor_ref[...] = anchor[32:96]
+    lit_ref[...] = in_ref[:, 32:160, :]
     for copy in copies[3:]:
         copy.wait()
 
 
-def weight_moves(turned_ref, first, out_ref, base):
+EARLY = 5
+
+
+def weight_moves(turned_ref, lines, out_ref, base):
     return [
-        (turned_ref.at[:, 128 * (first + n) : 128 * (first + n) + 128], out_ref.at[base + 64 * n : base + 64 * n + 64, :])
-        for n in range(9)
-    ]
-
-
-def second_kernel(sec_ref, teacher_ref, mid_ref, base_ref, steps_ref, turned_ref, out_ref, in_ref, sems):
-    copies = start_all(weight_moves(turned_ref, 0, out_ref, 128), sems)
+        (turned_ref.at[:, 128 * line : 128 * line + 128], out_ref.at[base + 64 * n : base + 64 * n + 64, :])
+        for n, line in enumerate(lines)
+    ]
+
+
+def second_kernel(
+    sec_ref, teacher_ref, student_ref, mid_ref, anchor_ref, lit_ref, steps_ref, fine_ref, turned_ref, out_ref, in_ref, sems
+):
+    moves = [
+        (fine_ref.at[:, 128 * n : 128 * n + 128], out_ref.at[128 + 256 * n : 384 + 256 * n, :]) for n in range(2)
+    ]
+    copies = start_all(moves + weight_moves(turned_ref, range(EARLY), out_ref, 640), sems)
     field = jnp.concatenate([sec_ref[s, 0:128, :] for s in range(4)], axis=1).astype(F32).reshape(4, 32, 512)
     for at, step in enumerate((-1, 0, 1)):
         in_ref[at] = shifted(field, step).astype(BF).reshape(128, 512)
@@ -182,9 +183,17 @@
             total += jnp.dot(
                 in_ref[dx, 32 * dy : 32 * dy + 64, :], teacher_ref[k : k + 512, :], preferred_element_type=F32
             )
-    target = mid_ref[...] + delta(steps_ref, 1) * total
+    pupil = jnp.zeros((64, 128), F32)
+    for dy in range(3):
+        for dx in range(3):
+            k = (3 * dy + dx) * 512
+            pupil += jnp.dot(
+                lit_ref[dx, 32 * dy : 32 * dy + 64, :], student_ref[k : k + 512, :], preferred_element_type=F32
+            )
+    one, two = delta(steps_ref, 0), delta(steps_ref, 1)
+    target = mid_ref[...] + two * total
     out_ref[0:64, :] = target.astype(BF)
-    out_ref[64:128, :] = (target - base_ref[...]).astype(BF)
+    out_ref[64:128, :] = (target - (anchor_ref[...] + (one + two) * pupil)).astype(BF)
     for copy in copies:
         copy.wait()
 
@@ -218,7 +227,15 @@
     for m in range(2):
         lift = lifted(target[32 * m : 32 * m + 32], proj)
         for i in range(4 * m, 4 * m + 4):
-            noisy = jnp.concatenate([near_ref[s, 192 + 32 * i : 224 + 32 * i, :] for s in range(4)], axis=0)
+            noisy = jnp.concatenate(
+                [
+                    jnp.concatenate(
+                        [late_ref[s, at + 32 * i : at + 32 * i + 32, :] for at in (128, 384)], axis=1
+                    )
+                    for s in range(4)
+                ],
+                axis=0,
+            )
             line_ref[128 * i : 128 * i + 128, :] = (noisy.astype(F32) + lift).astype(BF)
     begin = pl.multiple_of(32 * col, 32)
     before = pl.multiple_of(jnp.maximum(32 * col - 16, 0), 16)
@@ -226,8 +243,8 @@
     for i in range(8):
         for at, to, size in ((before, 0, 16), (begin, 16, 32), (after, 48, 16)):
             field_ref[i, to : to + size, :] = line_ref[pl.ds(128 * i + at, size), :]
-    one_ref[...] = jnp.where(even, line_ref[896:1024, :], line_ref[0:128, :])
-    two_ref[...] = jnp.where(even, line_ref[0:128, :], line_ref[896:1024, :])
+    one_ref[...] = jnp.where(even, field_ref[7], field_ref[0])
+    two_ref[...] = jnp.where(even, field_ref[0], field_ref[7])
     gap_scratch[...] = jnp.concatenate([late_ref[s, 64:128, :] for s in range(4)], axis=1).astype(F32)
     gap_ref[...] = jnp.concatenate(
         [gap_scratch[pl.ds(pl.multiple_of(32 * i + 8 * col, 8), 8), :] for i in range(2)], axis=0
@@ -239,14 +256,9 @@
     cot = jnp.concatenate(lines, axis=0).astype(F32)
     cot = jnp.where(col % 2 == 1, cot[:, 64:128], cot[:, 0:64]).reshape(10, 128, 64)
     moved = jnp.concatenate([shifted(cot, -dx) for dx in (-1, 0, 1)], axis=2).astype(BF).reshape(1280, 192)
-    field = line_ref[...]
+    field = line_ref[...].T
     for dy in (-1, 0, 1):
-        term = lax.dot_general(
-            field,
-            moved[(1 - dy) * 128 : (1 - dy) * 128 + 1024],
-            (((0,), (0,)), ((), ())),
-            preferred_element_type=F32,
-        )
+        term = jnp.dot(field, moved[(1 - dy) * 128 : (1 - dy) * 128 + 1024], preferred_element_type=F32)
         for dx in range(3):
             one = term[:, 64 * dx : 64 * dx + 64]
             at = (3 * (dy + 1) + dx) * 256
@@ -265,7 +277,7 @@
     for j in range(5):
         part_ref[:, :, 128 * j : 128 * j + 128] = jnp.stack([line(j), line(j + 5)], axis=1).astype(BF)
 def share_kernel(scale, part_ref, turned_ref, share_ref, sems):
-    copies = start_all(weight_moves(turned_ref, 9, share_ref, 32), sems)
+    copies = start_all(weight_moves(turned_ref, range(EARLY, 18), share_ref, 32), sems)
     total = jnp.sum(part_ref[...].astype(F32), axis=0) * scale
     rows = []
     for j in range(9):
@@ -289,11 +301,9 @@
     owned = [share_ref[s, 0:32, :].astype(F32) for s in range(4)]
     grad_ref[...] = jnp.concatenate([(own[:, 0:64] + own[:, 64:128])[0:18] for own in owned], axis=1)
     for s in range(4):
-        for n in range(9):
-            weight_ref[64 * s : 64 * s + 64, 128 * n : 128 * n + 128] = late_ref[s, 128 + 64 * n : 192 + 64 * n, :]
-            weight_ref[64 * s : 64 * s + 64, 1152 + 128 * n : 1280 + 128 * n] = share_ref[
-                s, 32 + 64 * n : 96 + 64 * n, :
-            ]
+        for n in range(18):
+            ref, at = (late_ref, 640 + 64 * n) if n < EARLY else (share_ref, 32 + 64 * (n - EARLY))
+            weight_ref[64 * s : 64 * s + 64, 128 * n : 128 * n + 128] = ref[s, at : at + 64, :]
     place = lax.broadcasted_iota(jnp.int32, (10, 64, 256), 1)
     framed = ((place >= 16) | (col > 0)) & ((place < 48) | (col < 3))
 
@@ -302,13 +312,9 @@
         for at in range(3):
             in_ref[at] = wide[:, 15 + at : 47 + at].astype(BF).reshape(320, 256)
 
-    begin = pl.multiple_of(32 * col, 32)
-    before = pl.multiple_of(jnp.maximum(32 * col - 16, 0), 16)
-    after = pl.multiple_of(jnp.minimum(32 * col + 32, 112), 16)
-    for at, to, size in ((before, 0, 16), (begin, 16, 32), (after, 48, 16)):
-        one, two = one_ref[pl.ds(at, size), :], two_ref[pl.ds(at, size), :]
-        tile_ref[0, to : to + size, :] = jnp.where(even, two, one)
-        tile_ref[9, to : to + size, :] = jnp.where(even, one, two)
+    one, two = one_ref[...], two_ref[...]
+    tile_ref[0] = jnp.where(even, two, one)
+    tile_ref[9] = jnp.where(even, one, two)
     tile_ref[1:9] = field_ref[...]
     lay_out()
     total = jnp.zeros((256, 256), F32)
@@ -357,7 +363,7 @@
         pack_kernel,
         [shape((64, 256), BF), shape((64, 256), BF)],
         [pltpu.SemaphoreType.DMA((6,))],
-        MIB,
+        20000 * MIB,
         56,
         "pack",
         [pl.ANY] * 2,
@@ -365,11 +371,11 @@
     two = lax.ppermute(two, "rows", far_pairs)
     pairs = [[i, i + 1] for i in range(0, count, 2)]
     one = lax.all_gather(one, "rows", axis=0, tiled=True, axis_index_groups=pairs)
-    near = lax.all_gather(jnp.concatenate([one, two, fine_noisy.reshape(256, 256)], axis=0), "cols", axis=0)
+    near = lax.all_gather(jnp.concatenate([one, two], axis=0), "cols", axis=0)
     steps = steps.reshape(1, 3)
-    sec, middle, base = call(
+    sec, middle, anchor, lit = call(
         first_kernel,
-        [shape((896, 128), BF), shape((64, 128), F32), shape((64, 128), F32)],
+        [shape((896, 128), BF), shape((64, 128), F32), shape((64, 128), F32), shape((3, 128, 512), BF)],
         [
             pltpu.VMEM((3, 4, 32, 256), BF),
             pltpu.VMEM((192, 512), F32),
@@ -380,26 +386,26 @@
         300 * MIB,
         16,
         "first",
-        [pl.ANY] + [pltpu.VMEM] * 3 + [pl.ANY] * 2,
-    )(near, teacher_weight, student_weight, steps, flat, projection.T)
+        [pl.ANY] + [pltpu.VMEM] * 2 + [pl.ANY] * 2,
+    )(near, teacher_weight, steps, flat, projection.T)
     sec = lax.all_gather(sec, "cols", axis=0)
     (late,) = call(
         second_kernel,
-        [shape((704, 128), BF)],
-        [pltpu.VMEM((3, 128, 512), BF), pltpu.SemaphoreType.DMA((9,))],
+        [shape((640 + 64 * EARLY, 128), BF)],
+        [pltpu.VMEM((3, 128, 512), BF), pltpu.SemaphoreType.DMA((2 + EARLY,))],
         100 * MIB,
         16,
         "second",
-        [pltpu.VMEM] * 5 + [pl.ANY],
-    )(sec, teacher_weight, middle, base, steps, turned)
+        [pltpu.VMEM] * 7 + [pl.ANY] * 2,
+    )(sec, teacher_weight, student_weight, middle, anchor, lit, steps, fine_noisy.reshape(256, 256), turned)
     late = lax.all_gather(late, "cols", axis=0)
     part, field, one, two, gap = call(
         grad_kernel,
         [
             shape((count, 2, 640), BF),
             shape((8, 64, 256), BF),
-            shape((128, 256), BF),
-            shape((128, 256), BF),
+            shape((64, 256), BF),
+            shape((64, 256), BF),
             shape((16, 512), BF),
         ],
         [pltpu.VMEM((1024, 256), BF), pltpu.VMEM((2304, 128), F32), pltpu.VMEM((64, 512), F32)],
@@ -413,8 +419,8 @@
     one = lax.ppermute(one, "rows", near_pairs)
     (share,) = call(
         functools.partial(share_kernel, 1.0 / math.sqrt(1024 * count)),
-        [shape((608, 128), BF)],
-        [pltpu.SemaphoreType.DMA((9,))],
+        [shape((32 + 64 * (18 - EARLY), 128), BF)],
+        [pltpu.SemaphoreType.DMA((18 - EARLY,))],
         MIB,
         8,
         "share",

time: 97.9 us -> 95.5 us (0.975)
  local copies, waits for them, and re-layouts: 1.99 us -> 0.04 us
  blocking collectives: 46.8 us -> 47.8 us
    all_gather x1, blocking collectives: 13.1 us -> 10.9 us  [on_device(): near = lax.all_gather(jnp.concatenate([one, two], axis=0), 'cols', axis=0)]
    unnamed x16 -> x14, local copies, waits for them, and re-layouts: 1.99 us -> 0.04 us
    all_gather x1, blocking collectives: 9.01 us -> 10.9 us  [on_device(): share = lax.all_gather(share, 'cols', axis=0)]
    all_gather x1, blocking collectives: 8.36 us -> 9.79 us  [on_device(): late = lax.all_gather(late, 'cols', axis=0)]
where the time goes in v3:
time: 95.5 us; the launch traced here: 95.2 us
  blocking collectives  47.8 us (50%)
  starting transfers between devices  24.1 us (25%)
  waiting for transfers between devices  14.5 us (15%)
  Pallas kernels  7.92 us (8%)
    all_to_all x1, starting transfers between devices, on_device(): part = lax.all_to_all(part, 'rows', 0, 0, tiled=True)  20.3 us
    all_to_all x1, waiting for transfers between devices, on_device(): part = lax.all_to_all(part, 'rows', 0, 0, tiled=True)  14.5 us
    all_gather x1, blocking collectives, on_device(): near = lax.all_gather(jnp.concatenate([one, two], axis=0), 'cols', axis=0)  10.9 us
    all_gather x1, blocking collectives, on_device(): share = lax.all_gather(share, 'cols', axis=0)  10.9 us
    all_gather x1, blocking collectives, on_device(): late = lax.all_gather(late, 'cols', axis=0)  9.79 us
    all_gather x1, blocking collectives, on_device(): sec = lax.all_gather(sec, 'cols', axis=0)  9.43 us
    all_gather x1, blocking collectives, on_device(): lax.all_gather(one, 'rows', axis=0, tiled=True, axis_index_groups=pairs)  6.73 us
    pallas_call x1, Pallas kernels, on_device(): call(grad_kernel, [shape((count, 2, 640), BF), shape((8, 64, 256), BF), s...  2.6 us
  transfers between devices with their start and end apart: 4, of which 1 were waited for; matrix products, arithmetic and copies ran while one was open for 0% of the time, Pallas kernels for 1%

profile of v3, /device:TPU:1, one launch (start us, length us, event | category | flops | bytes accessed | tf_op | source)
XLA Modules:
  0.0 95.2 jit_solution(6557220980537683093)
XLA Ops:
  0.6 0.0 copy-start
  0.6 0.0 copy-start.4
  0.7 0.0 copy-start.5
  0.7 0.0 copy-start.6
  0.7 1.6 %pack.1 = (bf16[64,256]{1,0:T(8,128)(2,1)}, bf16[64,256]{1,0:T(8,128)(2,1)}) custom-call(bf16[256,256]{1,0:T(8,128)(2,1)} %bitcast.25, bf16[16,512]{1,0:T(8,128)(2,1)} %bitcast.30), custom_call_target="tpu_custom_call" | custom-call | flops 20971520000 | bytes 1048576 | tf_op jit(solution)/shard_map/pack/pallas_call | solution.py:362
  2.2 0.7 collective-permute-start
  2.9 6.7 %all_gather.27 = bf16[128,256]{1,0:T(8,128)(2,1)S(1)} all-gather(bf16[64,256]{1,0:T(8,128)(2,1)} %get-tuple-element.21), channel_id=1, replica_groups={{0,4},{8,12},{16,20},{24,28},{32,36},{40,44},{48,52},{56,60},{64,68},{7..., dimensions={0}, use_global_device_ids=true | all-gather | bytes 98304 | tf_op jit(solution)/shard_map/all_gather | solution.py:373
  9.6 0.0 collective-permute-done
  9.7 10.9 %all-gather = bf16[768,256]{1,0:T(8,128)(2,1)S(1)} all-gather(bf16[192,256]{1,0:T(8,128)(2,1)S(1)} %pad_maximum_fusion), channel_id=2, replica_groups=mesh['rows'=128,'cols'=4] {'cols'}, dimensions={0}, use_global_device_ids=true | all-gather | bytes 491520 | tf_op jit(solution)/shard_map/all_gather | solution.py:374
  20.6 0.0 copy-done
  20.6 0.0 copy-done.4
  20.6 0.0 copy-done.5
  20.6 0.0 copy-done.6
  20.6 0.0 copy-start.1
  20.6 0.0 copy-start.2
  20.7 0.0 copy-start.3
  20.7 0.9 first.1
  21.6 9.4 %all-gather.1 = bf16[3584,128]{1,0:T(8,128)(2,1)S(1)} all-gather(bf16[896,128]{1,0:T(8,128)(2,1)S(1)} %get-tuple-element.23), channel_id=3, replica_groups=mesh['rows'=128,'cols'=4] {'cols'}, dimensions={0}, use_global_device_ids=true | all-gather | bytes 1146880 | tf_op jit(solution)/shard_map/all_gather | solution.py:391
  31.0 0.0 copy-done.1
  31.0 0.0 copy-done.2
  31.0 0.0 copy-done.3
  31.0 0.6 second.1
  31.6 9.8 %all-gather.2 = bf16[3840,128]{1,0:T(8,128)(2,1)S(1)} all-gather(bf16[960,128]{1,0:T(8,128)(2,1)S(1)} %second.1), channel_id=4, replica_groups=mesh['rows'=128,'cols'=4] {'cols'}, dimensions={0}, use_global_device_ids=true | all-gather | bytes 1228800 | tf_op jit(solution)/shard_map/all_gather | solution.py:401
  41.4 2.6 %grad.1 = (bf16[128,2,640]{2,1,0:T(2,128)(2,1)}, bf16[8,64,256]{2,1,0:T(8,128)(2,1)S(1)}, bf16[64,256]{1,0:T(8,128)(2,1)S(1)}, bf16[64,256]{1,0:T(8,128)(2,1)S(1)}, bf16[16,512]{1,0:T(8,128)(2,1)}) custom-call(bf16[4,192,256]{2,1,0:T(8,128)(2,1)S(1)} %bitcast.17, bf16[4,896,128]{2,1,0:T(8,128)(2,1)S(1)} %bitcast.14, bf16[4,960,128]{2,1,0:T(8,128)(2,1)S(1)} %bitcast.21), custom_call_target="tpu_custom_call" | custom-call | flops 1048576000 | bytes 1048576 | tf_op jit(solution)/shard_map/grad/pallas_call | solution.py:402
  44.0 20.3 %all-to-all-start = ((bf16[128,2,640]{2,1,0:T(2,128)(2,1)}), bf16[128,2,640]{2,1,0:T(2,128)(2,1)S(1)}, u32[]{:S(2)}, u32[]{:S(2)}) async-start(bf16[128,2,640]{2,1,0:T(2,128)(2,1)} %get-tuple-element.27), calls=%async_computation | async-start | bytes 655360 | tf_op jit(solution)/shard_map/all_to_all | solution.py:417
  64.3 2.5 %collective-permute-start.1 = (bf16[64,256]{1,0:T(8,128)(2,1)S(1)}, bf16[64,256]{1,0:T(8,128)(2,1)S(1)}, u32[]{:S(2)}, u32[]{:S(2)}) collective-permute-start(bf16[64,256]{1,0:T(8,128)(2,1)S(1)} %get-tuple-element.28), channel_id=1, source_target_pairs={{4,0},{0,4},{12,8},{8,12},{20,16},{16,20},{28,24},{24,28},{36,32},... | collective-permute-start | bytes 98312 | tf_op jit(solution)/shard_map/ppermute | solution.py:419
  66.8 0.7 collective-permute-start.2
  67.5 14.5 %all-to-all-done.part_ref = bf16[128,2,640]{2,1,0:T(2,128)(2,1)S(1)} async-done(((bf16[128,2,640]{2,1,0:T(2,128)(2,1)}), bf16[128,2,640]{2,1,0:T(2,128)(2,1)S(1)}, u32[]{:S(2)}, u32[]{:S(2)}) %all-to-all-start) | async-done | bytes 327712 | tf_op jit(solution)/shard_map/all_to_all | solution.py:417
  82.0 0.7 share.1
  82.7 10.9 %all-gather.3 = bf16[3456,128]{1,0:T(8,128)(2,1)S(1)} all-gather(bf16[864,128]{1,0:T(8,128)(2,1)S(1)} %share.1), channel_id=5, replica_groups=mesh['rows'=128,'cols'=4] {'cols'}, dimensions={0}, use_global_device_ids=true | all-gather | bytes 1105920 | tf_op jit(solution)/shard_map/all_gather | solution.py:429
  93.6 0.0 collective-permute-done.1.one_ref
  93.6 0.0 collective-permute-done.2.two_ref
  93.6 1.5 %fine.1 = (bf16[256,256]{1,0:T(8,128)(2,1)}, bf16[256,256]{1,0:T(8,128)(2,1)}, f32[18,256]{1,0:T(8,128)}) custom-call(bf16[4,192,256]{2,1,0:T(8,128)(2,1)S(1)} %bitcast.18, bf16[4,896,128]{2,1,0:T(8,128)(2,1)S(1)} %bitcast.15, bf16[4,960,128]{2,1,0:T(8,128)(2,1)S(1)} %bitcast.22, bf16[4,864,128]{2,1,0:T(8,128)(2,1)S(1)} %bitcast.23, ...), custom_call_target="tpu_custom_call" | custom-call | flops 1048576000 | bytes 1048576 | tf_op jit(solution)/shard_map/fine/pallas_call | solution.py:431
  (1 shorter events, 0.0 us)
Async XLA Ops:
  0.6 20.0 %copy-start = (bf16[4608,128]{1,0:T(8,128)(2,1)S(1)}, bf16[4608,128]{1,0:T(8,128)(2,1)}, u32[]{:S(2)}) copy-start(bf16[4608,128]{1,0:T(8,128)(2,1)} %teacher_ref.3) | copy-start | bytes 3538948
  0.6 20.0 %copy-start.4 = (bf16[8,32,256]{2,1,0:T(8,128)(2,1)S(1)}, bf16[8,32,256]{2,1,0:T(8,128)(2,1)}, u32[]{:S(2)}) copy-start(bf16[8,32,256]{2,1,0:T(8,128)(2,1)} %param.15) | copy-start | bytes 393220
  0.7 20.0 %copy-start.5 = (bf16[512,64]{0,1:T(8,128)(2,1)S(1)}, bf16[512,64]{0,1:T(8,128)(2,1)}, u32[]{:S(2)}) copy-start(bf16[512,64]{0,1:T(8,128)(2,1)} %param.10) | copy-start | bytes 196612
  0.7 20.0 %copy-start.6 = (s32[3]{0:T(128)S(1)}, s32[3]{0:T(128)}, u32[]{:S(2)}) copy-start(s32[3]{0:T(128)} %param.14) | copy-start | bytes 40
  2.2 7.4 %collective-permute-start = (bf16[64,256]{1,0:T(8,128)(2,1)}, bf16[64,256]{1,0:T(8,128)(2,1)S(1)}, u32[]{:S(2)}, u32[]{:S(2)}) collective-permute-start(bf16[64,256]{1,0:T(8,128)(2,1)} %get-tuple-element.22), channel_id=1, source_target_pairs={{4,8},{8,4},{12,16},{16,12},{20,24},{24,20},{28,32},{32,28},{36,40... | collective-permute-start | bytes 98312 | tf_op jit(solution)/shard_map/ppermute | solution.py:371
  20.6 10.4 %copy-start.1 = (bf16[2304,64]{0,1:T(8,128)(2,1)S(1)}, bf16[2304,64]{0,1:T(8,128)(2,1)}, u32[]{:S(2)}) copy-start(bf16[2304,64]{0,1:T(8,128)(2,1)} %param.9) | copy-start | bytes 884740
  20.6 10.3 %copy-start.2 = (bf16[4608,128]{1,0:T(8,128)(2,1)S(1)}, bf16[4608,128]{1,0:T(8,128)(2,1)}, u32[]{:S(2)}) copy-start(bf16[4608,128]{1,0:T(8,128)(2,1)} %student_ref.1) | copy-start | bytes 3538948
  20.7 10.3 %copy-start.3 = (bf16[8,32,256]{2,1,0:T(8,128)(2,1)S(1)}, bf16[8,32,256]{2,1,0:T(8,128)(2,1)}, u32[]{:S(2)}) copy-start(bf16[8,32,256]{2,1,0:T(8,128)(2,1)} %param.8) | copy-start | bytes 393220
  44.0 37.9 %all-to-all-start = ((bf16[128,2,640]{2,1,0:T(2,128)(2,1)}), bf16[128,2,640]{2,1,0:T(2,128)(2,1)S(1)}, u32[]{:S(2)}, u32[]{:S(2)}) async-start(bf16[128,2,640]{2,1,0:T(2,128)(2,1)} %get-tuple-element.27), calls=%async_computation | async-start | bytes 655360 | tf_op jit(solution)/shard_map/all_to_all | solution.py:417
  64.3 29.3 %collective-permute-start.1 = (bf16[64,256]{1,0:T(8,128)(2,1)S(1)}, bf16[64,256]{1,0:T(8,128)(2,1)S(1)}, u32[]{:S(2)}, u32[]{:S(2)}) collective-permute-start(bf16[64,256]{1,0:T(8,128)(2,1)S(1)} %get-tuple-element.28), channel_id=1, source_target_pairs={{4,0},{0,4},{12,8},{8,12},{20,16},{16,20},{28,24},{24,28},{36,32},... | collective-permute-start | bytes 98312 | tf_op jit(solution)/shard_map/ppermute | solution.py:419
  66.8 26.8 %collective-permute-start.2 = (bf16[64,256]{1,0:T(8,128)(2,1)S(1)}, bf16[64,256]{1,0:T(8,128)(2,1)S(1)}, u32[]{:S(2)}, u32[]{:S(2)}) collective-permute-start(bf16[64,256]{1,0:T(8,128)(2,1)S(1)} %get-tuple-element.29), channel_id=1, source_target_pairs={{4,8},{8,4},{12,16},{16,12},{20,24},{24,20},{28,32},{32,28},{36,40... | collective-permute-start | bytes 98312 | tf_op jit(solution)/shard_map/ppermute | solution.py:418

commit v4 on v3

--- a/solution.py
+++ b/solution.py
@@ -156,23 +156,13 @@
         copy.wait()
 
 
-EARLY = 5
-
-
-def weight_moves(turned_ref, lines, out_ref, base):
-    return [
-        (turned_ref.at[:, 128 * line : 128 * line + 128], out_ref.at[base + 64 * n : base + 64 * n + 64, :])
-        for n, line in enumerate(lines)
-    ]
-
-
 def second_kernel(
-    sec_ref, teacher_ref, student_ref, mid_ref, anchor_ref, lit_ref, steps_ref, fine_ref, turned_ref, out_ref, in_ref, sems
+    sec_ref, teacher_ref, student_ref, mid_ref, anchor_ref, lit_ref, steps_ref, fine_ref, out_ref, in_ref, sems
 ):
     moves = [
         (fine_ref.at[:, 128 * n : 128 * n + 128], out_ref.at[128 + 256 * n : 384 + 256 * n, :]) for n in range(2)
     ]
-    copies = start_all(moves + weight_moves(turned_ref, range(EARLY), out_ref, 640), sems)
+    copies = start_all(moves, sems)
     field = jnp.concatenate([sec_ref[s, 0:128, :] for s in range(4)], axis=1).astype(F32).reshape(4, 32, 512)
     for at, step in enumerate((-1, 0, 1)):
         in_ref[at] = shifted(field, step).astype(BF).reshape(128, 512)
@@ -276,8 +266,7 @@
 
     for j in range(5):
         part_ref[:, :, 128 * j : 128 * j + 128] = jnp.stack([line(j), line(j + 5)], axis=1).astype(BF)
-def share_kernel(scale, part_ref, turned_ref, share_ref, sems):
-    copies = start_all(weight_moves(turned_ref, range(EARLY, 18), share_ref, 32), sems)
+def share_kernel(scale, part_ref, share_ref):
     total = jnp.sum(part_ref[...].astype(F32), axis=0) * scale
     rows = []
     for j in range(9):
@@ -285,13 +274,11 @@
         rows += [line[:, 0:64], line[:, 64:128]]
     own = jnp.concatenate(rows + [jnp.zeros((14, 64), F32)], axis=0)
     high = own.astype(BF).astype(F32)
-    share_ref[0:32, :] = jnp.concatenate([high, own - high], axis=1).astype(BF)
-    for copy in copies:
-        copy.wait()
+    share_ref[...] = jnp.concatenate([high, own - high], axis=1).astype(BF)
 
 
 def fine_kernel(
-    near_ref, sec_ref, late_ref, share_ref, field_ref, one_ref, two_ref,
+    near_ref, sec_ref, turned_ref, beside_ref, across_ref, corner_ref, share_ref, field_ref, one_ref, two_ref,
     out_ref, back_ref, grad_ref,
     weight_ref, tile_ref, in_ref,
 ):
@@ -300,10 +287,9 @@
     above, below, _ = near_at(row)
     owned = [share_ref[s, 0:32, :].astype(F32) for s in range(4)]
     grad_ref[...] = jnp.concatenate([(own[:, 0:64] + own[:, 64:128])[0:18] for own in owned], axis=1)
-    for s in range(4):
-        for n in range(18):
-            ref, at = (late_ref, 640 + 64 * n) if n < EARLY else (share_ref, 32 + 64 * (n - EARLY))
-            weight_ref[64 * s : 64 * s + 64, 128 * n : 128 * n + 128] = ref[s, at : at + 64, :]
+    for k, block in enumerate((turned_ref, beside_ref, across_ref, corner_ref)):
+        tile = jnp.bitwise_xor(col, k)
+        weight_ref[pl.ds(pl.multiple_of(64 * tile, 64), 64), :] = block[...]
     place = lax.broadcasted_iota(jnp.int32, (10, 64, 256), 1)
     framed = ((place >= 16) | (col > 0)) & ((place < 48) | (col < 3))
 
@@ -357,7 +343,6 @@
     near_pairs = [(i ^ 1, i) for i in range(count)]
     far_pairs = [(i, i + 1 if i % 2 else i - 1) for i in range(1, count - 1)]
 
-    turned = fine_weight.T
     flat = cotangent.reshape(256, 256)
     one, two = call(
         pack_kernel,
@@ -391,13 +376,13 @@
     sec = lax.all_gather(sec, "cols", axis=0)
     (late,) = call(
         second_kernel,
-        [shape((640 + 64 * EARLY, 128), BF)],
-        [pltpu.VMEM((3, 128, 512), BF), pltpu.SemaphoreType.DMA((2 + EARLY,))],
+        [shape((640, 128), BF)],
+        [pltpu.VMEM((3, 128, 512), BF), pltpu.SemaphoreType.DMA((2,))],
         100 * MIB,
         16,
         "second",
-        [pltpu.VMEM] * 7 + [pl.ANY] * 2,
-    )(sec, teacher_weight, student_weight, middle, anchor, lit, steps, fine_noisy.reshape(256, 256), turned)
+        [pltpu.VMEM] * 7 + [pl.ANY],
+    )(sec, teacher_weight, student_weight, middle, anchor, lit, steps, fine_noisy.reshape(256, 256))
     late = lax.all_gather(late, "cols", axis=0)
     part, field, one, two, gap = call(
         grad_kernel,
@@ -414,18 +399,23 @@
         "grad",
         [pltpu.VMEM] * 3,
     )(near, sec, late)
+    turned, one, two, part = lax.optimization_barrier((fine_weight.T, one, two, part))
     part = lax.all_to_all(part, "rows", 0, 0, tiled=True)
+    across = lax.ppermute(turned, "cols", [(i, i ^ 2) for i in range(4)])
+    beside = lax.ppermute(turned, "cols", [(i, i ^ 1) for i in range(4)])
     two = lax.ppermute(two, "rows", far_pairs)
     one = lax.ppermute(one, "rows", near_pairs)
+    across, one, two = lax.optimization_barrier((across, one, two))
+    corner = lax.ppermute(across, "cols", [(i, i ^ 1) for i in range(4)])
     (share,) = call(
         functools.partial(share_kernel, 1.0 / math.sqrt(1024 * count)),
-        [shape((32 + 64 * (18 - EARLY), 128), BF)],
-        [pltpu.SemaphoreType.DMA((18 - EARLY,))],
+        [shape((32, 128), BF)],
+        [],
         MIB,
         8,
         "share",
-        [pltpu.VMEM, pl.ANY],
-    )(part, turned)
+        [pltpu.VMEM],
+    )(part)
     share = lax.all_gather(share, "cols", axis=0)
     share, one, two = lax.optimization_barrier((share, one, two))
     fine_out, grad_input, grad_weight = call(
@@ -435,8 +425,8 @@
         1000 * MIB,
         32,
         "fine",
-        [pltpu.VMEM] * 7,
-    )(near, sec, late, share, field, one, two)
+        [pltpu.VMEM] * 10,
+    )(near, sec, turned, beside, across, corner, share, field, one, two)
     return (
         fine_out.reshape(8, 32, 256),
         grad_input.reshape(8, 32, 256),

time: 95.5 us -> 90 us (0.942)
  starting transfers between devices: 24.1 us -> 32.7 us
  blocking collectives: 47.8 us -> 40.2 us
  waiting for transfers between devices: 14.5 us -> 8.01 us
    all_to_all x1, waiting for transfers between devices: 14.5 us -> 0.01 us  [on_device(): part = lax.all_to_all(part, 'rows', 0, 0, tiled=True)]
    ppermute x0 -> x3, starting transfers between devices: none -> 8.61 us  [the longest x1 3.19 us: on_device(): beside = lax.ppermute(turned, 'cols', [(i, i ^ 1) for i in range(4)])]
    ppermute x0 -> x3, waiting for transfers between devices: none -> 8 us  [the longest x1 8 us: on_device(): across = lax.ppermute(turned, 'cols', [(i, i ^ 2) for i in range(4)])]
    all_gather x1, blocking collectives: 10.9 us -> 5.06 us  [on_device(): share = lax.all_gather(share, 'cols', axis=0)]
    all_gather x1, blocking collectives: 9.79 us -> 8.01 us  [on_device(): late = lax.all_gather(late, 'cols', axis=0)]
  transfers between devices with their start and end apart: 4 -> 7, of which waited for: 1 -> 1; matrix products, arithmetic and copies ran while one was open for 0% -> 0% of each run, Pallas kernels for 1% -> 1%
where the time goes in v4:
time: 90 us; the launch traced here: 89.5 us
  blocking collectives  40.2 us (45%)
  starting transfers between devices  32.7 us (36%)
  waiting for transfers between devices  8.01 us (9%)
  Pallas kernels  7.71 us (9%)
    all_to_all x1, starting transfers between devices, on_device(): part = lax.all_to_all(part, 'rows', 0, 0, tiled=True)  20.3 us
    all_gather x1, blocking collectives, on_device(): near = lax.all_gather(jnp.concatenate([one, two], axis=0), 'cols', axis=0)  10.9 us
    all_gather x1, blocking collectives, on_device(): sec = lax.all_gather(sec, 'cols', axis=0)  9.43 us
    all_gather x1, blocking collectives, on_device(): late = lax.all_gather(late, 'cols', axis=0)  8.01 us
    ppermute x1, waiting for transfers between devices, on_device(): across = lax.ppermute(turned, 'cols', [(i, i ^ 2) for i in range(4)])  8 us
    all_gather x1, blocking collectives, on_device(): lax.all_gather(one, 'rows', axis=0, tiled=True, axis_index_groups=pairs)  6.73 us
    all_gather x1, blocking collectives, on_device(): share = lax.all_gather(share, 'cols', axis=0)  5.06 us
    ppermute x1, starting transfers between devices, on_device(): beside = lax.ppermute(turned, 'cols', [(i, i ^ 1) for i in range(4)])  3.19 us
  transfers between devices with their start and end apart: 7, of which 1 were waited for; matrix products, arithmetic and copies ran while one was open for 0% of the time, Pallas kernels for 1%

profile of v4, /device:TPU:1, one launch (start us, length us, event | category | flops | bytes accessed | tf_op | source)
XLA Modules:
  0.0 89.5 jit_solution(6178189595506679833)
XLA Ops:
  0.6 0.0 copy-start
  0.6 0.0 copy-start.3
  0.7 0.0 copy-start.4
  0.7 0.0 copy-start.5
  0.7 1.6 %pack.1 = (bf16[64,256]{1,0:T(8,128)(2,1)}, bf16[64,256]{1,0:T(8,128)(2,1)}) custom-call(bf16[256,256]{1,0:T(8,128)(2,1)} %bitcast.21, bf16[16,512]{1,0:T(8,128)(2,1)} %bitcast.30), custom_call_target="tpu_custom_call" | custom-call | flops 20971520000 | bytes 1048576 | tf_op jit(solution)/shard_map/pack/pallas_call | solution.py:347
  2.2 0.7 collective-permute-start
  2.9 6.7 %all_gather.27 = bf16[128,256]{1,0:T(8,128)(2,1)S(1)} all-gather(bf16[64,256]{1,0:T(8,128)(2,1)} %get-tuple-element.28), channel_id=1, replica_groups={{0,4},{8,12},{16,20},{24,28},{32,36},{40,44},{48,52},{56,60},{64,68},{7..., dimensions={0}, use_global_device_ids=true | all-gather | bytes 98304 | tf_op jit(solution)/shard_map/all_gather | solution.py:358
  9.6 0.0 collective-permute-done
  9.7 10.9 %all-gather = bf16[768,256]{1,0:T(8,128)(2,1)S(1)} all-gather(bf16[192,256]{1,0:T(8,128)(2,1)S(1)} %pad_maximum_fusion), channel_id=2, replica_groups=mesh['rows'=128,'cols'=4] {'cols'}, dimensions={0}, use_global_device_ids=true | all-gather | bytes 491520 | tf_op jit(solution)/shard_map/all_gather | solution.py:359
  20.6 0.0 copy-done
  20.6 0.0 copy-done.3
  20.6 0.0 copy-done.4
  20.6 0.0 copy-done.5
  20.6 0.0 copy-start.1
  20.6 0.0 copy-start.2
  20.7 0.9 first.1
  21.5 9.4 %all-gather.1 = bf16[3584,128]{1,0:T(8,128)(2,1)S(1)} all-gather(bf16[896,128]{1,0:T(8,128)(2,1)S(1)} %get-tuple-element.30), channel_id=3, replica_groups=mesh['rows'=128,'cols'=4] {'cols'}, dimensions={0}, use_global_device_ids=true | all-gather | bytes 1146880 | tf_op jit(solution)/shard_map/all_gather | solution.py:376
  31.0 0.0 copy-done.1
  31.0 0.0 copy-done.2
  31.0 0.6 second.1
  31.6 8.0 %all-gather.2 = bf16[2560,128]{1,0:T(8,128)(2,1)S(1)} all-gather(bf16[640,128]{1,0:T(8,128)(2,1)S(1)} %second.1), channel_id=4, replica_groups=mesh['rows'=128,'cols'=4] {'cols'}, dimensions={0}, use_global_device_ids=true | all-gather | bytes 819200 | tf_op jit(solution)/shard_map/all_gather | solution.py:386
  39.6 0.0 copy-start.6
  39.6 2.6 %grad.1 = (bf16[128,2,640]{2,1,0:T(2,128)(2,1)}, bf16[8,64,256]{2,1,0:T(8,128)(2,1)S(1)}, bf16[64,256]{1,0:T(8,128)(2,1)S(1)}, bf16[64,256]{1,0:T(8,128)(2,1)S(1)}, bf16[16,512]{1,0:T(8,128)(2,1)}) custom-call(bf16[4,192,256]{2,1,0:T(8,128)(2,1)S(1)} %bitcast.17, bf16[4,896,128]{2,1,0:T(8,128)(2,1)S(1)} %bitcast.14, bf16[4,640,128]{2,1,0:T(8,128)(2,1)S(1)} %bitcast.19), custom_call_target="tpu_custom_call" | custom-call | flops 1048576000 | bytes 1048576 | tf_op jit(solution)/shard_map/grad/pallas_call | solution.py:387
  42.2 20.3 %all-to-all-start = ((bf16[128,2,640]{2,1,0:T(2,128)(2,1)}), bf16[128,2,640]{2,1,0:T(2,128)(2,1)S(1)}, u32[]{:S(2)}, u32[]{:S(2)}) async-start(bf16[128,2,640]{2,1,0:T(2,128)(2,1)} %get-tuple-element.41), calls=%async_computation | async-start | bytes 655360 | tf_op jit(solution)/shard_map/all_to_all | solution.py:403
  62.5 0.0 copy-done.6
  62.5 2.8 %collective-permute-start.2 = (bf16[64,2304]{1,0:T(8,128)(2,1)S(1)}, bf16[64,2304]{1,0:T(8,128)(2,1)S(1)}, u32[]{:S(2)}, u32[]{:S(2)}) collective-permute-start(bf16[64,2304]{1,0:T(8,128)(2,1)S(1)} %bitcast.27), channel_id=1, source_target_pairs={{0,2},{1,3},{2,0},{3,1},{4,6},{5,7},{6,4},{7,5},{8,10},{9,11},{10,... | collective-permute-start | bytes 884744 | tf_op jit(solution)/shard_map/ppermute | solution.py:404
  65.3 2.5 %collective-permute-start.3 = (bf16[64,256]{1,0:T(8,128)(2,1)S(1)}, bf16[64,256]{1,0:T(8,128)(2,1)S(1)}, u32[]{:S(2)}, u32[]{:S(2)}) collective-permute-start(bf16[64,256]{1,0:T(8,128)(2,1)S(1)} %get-tuple-element.38), channel_id=1, source_target_pairs={{4,0},{0,4},{12,8},{8,12},{20,16},{16,20},{28,24},{24,28},{36,32},... | collective-permute-start | bytes 98312 | tf_op jit(solution)/shard_map/ppermute | solution.py:407
  67.8 0.7 collective-permute-start.4
  68.4 3.2 %collective-permute-start.1 = (bf16[64,2304]{1,0:T(8,128)(2,1)S(1)}, bf16[64,2304]{1,0:T(8,128)(2,1)S(1)}, u32[]{:S(2)}, u32[]{:S(2)}) collective-permute-start(bf16[64,2304]{1,0:T(8,128)(2,1)S(1)} %bitcast.28), channel_id=1, source_target_pairs={{0,1},{1,0},{2,3},{3,2},{4,5},{5,4},{6,7},{7,6},{8,9},{9,8},{10,11... | collective-permute-start | bytes 884744 | tf_op jit(solution)/shard_map/ppermute | solution.py:405
  71.6 0.0 collective-permute-done.3.one_ref
  71.7 0.0 collective-permute-done.4.two_ref
  71.7 8.0 %collective-permute-done.2.across_ref = bf16[64,2304]{1,0:T(8,128)(2,1)S(1)} collective-permute-done((bf16[64,2304]{1,0:T(8,128)(2,1)S(1)}, bf16[64,2304]{1,0:T(8,128)(2,1)S(1)}, u32[]{:S(2)}, u32[]{:S(2)}) %collective-permute-start.2) | collective-permute-done | bytes 294944 | tf_op jit(solution)/shard_map/ppermute | solution.py:404
  79.7 2.6 %collective-permute-start.5 = (bf16[64,2304]{1,0:T(8,128)(2,1)S(1)}, bf16[64,2304]{1,0:T(8,128)(2,1)S(1)}, u32[]{:S(2)}, u32[]{:S(2)}) collective-permute-start(bf16[64,2304]{1,0:T(8,128)(2,1)S(1)} %collective-permute-done.2.across_ref), channel_id=1, source_target_pairs={{0,1},{1,0},{2,3},{3,2},{4,5},{5,4},{6,7},{7,6},{8,9},{9,8},{10,11... | collective-permute-start | bytes 884744 | tf_op jit(solution)/shard_map/ppermute | solution.py:409
  82.3 0.0 all-to-all-done.part_ref
  82.3 0.5 share.1
  82.8 5.1 %all-gather.3 = bf16[128,128]{1,0:T(8,128)(2,1)S(1)} all-gather(bf16[32,128]{1,0:T(8,128)(2,1)S(1)} %share.1), channel_id=5, replica_groups=mesh['rows'=128,'cols'=4] {'cols'}, dimensions={0}, use_global_device_ids=true | all-gather | bytes 40960 | tf_op jit(solution)/shard_map/all_gather | solution.py:419
  87.9 0.0 collective-permute-done.1.beside_ref
  87.9 0.0 collective-permute-done.5.corner_ref
  87.9 1.6 %fine.1 = (bf16[256,256]{1,0:T(8,128)(2,1)}, bf16[256,256]{1,0:T(8,128)(2,1)}, f32[18,256]{1,0:T(8,128)}) custom-call(bf16[4,192,256]{2,1,0:T(8,128)(2,1)S(1)} %bitcast.18, bf16[4,896,128]{2,1,0:T(8,128)(2,1)S(1)} %bitcast.15, bf16[64,2304]{1,0:T(8,128)(2,1)S(1)} %bitcast.29, bf16[64,2304]{1,0:T(8,128)(2,1)S(1)} %collective-permute-done.1.beside_ref, ...), custom_call_target="tpu_custom_call" | custom-call | flops 1048576000 | bytes 1048576 | tf_op jit(solution)/shard_map/fine/pallas_call | solution.py:421
  (1 shorter events, 0.0 us)
Async XLA Ops:
  0.6 20.0 %copy-start = (bf16[4608,128]{1,0:T(8,128)(2,1)S(1)}, bf16[4608,128]{1,0:T(8,128)(2,1)}, u32[]{:S(2)}) copy-start(bf16[4608,128]{1,0:T(8,128)(2,1)} %teacher_ref.3) | copy-start | bytes 3538948
  0.6 20.0 %copy-start.3 = (bf16[8,32,256]{2,1,0:T(8,128)(2,1)S(1)}, bf16[8,32,256]{2,1,0:T(8,128)(2,1)}, u32[]{:S(2)}) copy-start(bf16[8,32,256]{2,1,0:T(8,128)(2,1)} %param.15) | copy-start | bytes 393220
  0.7 20.0 %copy-start.4 = (bf16[512,64]{0,1:T(8,128)(2,1)S(1)}, bf16[512,64]{0,1:T(8,128)(2,1)}, u32[]{:S(2)}) copy-start(bf16[512,64]{0,1:T(8,128)(2,1)} %param.10) | copy-start | bytes 196612
  0.7 20.0 %copy-start.5 = (s32[3]{0:T(128)S(1)}, s32[3]{0:T(128)}, u32[]{:S(2)}) copy-start(s32[3]{0:T(128)} %param.14) | copy-start | bytes 40
  2.2 7.4 %collective-permute-start = (bf16[64,256]{1,0:T(8,128)(2,1)}, bf16[64,256]{1,0:T(8,128)(2,1)S(1)}, u32[]{:S(2)}, u32[]{:S(2)}) collective-permute-start(bf16[64,256]{1,0:T(8,128)(2,1)} %get-tuple-element.29), channel_id=1, source_target_pairs={{4,8},{8,4},{12,16},{16,12},{20,24},{24,20},{28,32},{32,28},{36,40... | collective-permute-start | bytes 98312 | tf_op jit(solution)/shard_map/ppermute | solution.py:356
  20.6 10.3 %copy-start.1 = (bf16[4608,128]{1,0:T(8,128)(2,1)S(1)}, bf16[4608,128]{1,0:T(8,128)(2,1)}, u32[]{:S(2)}) copy-start(bf16[4608,128]{1,0:T(8,128)(2,1)} %student_ref.1) | copy-start | bytes 3538948
  20.6 10.3 %copy-start.2 = (bf16[8,32,256]{2,1,0:T(8,128)(2,1)S(1)}, bf16[8,32,256]{2,1,0:T(8,128)(2,1)}, u32[]{:S(2)}) copy-start(bf16[8,32,256]{2,1,0:T(8,128)(2,1)} %param.8) | copy-start | bytes 393220
  39.6 22.9 %copy-start.6 = (bf16[2304,64]{0,1:T(8,128)(2,1)S(1)}, bf16[2304,64]{0,1:T(8,128)(2,1)}, u32[]{:S(2)}) copy-start(bf16[2304,64]{0,1:T(8,128)(2,1)} %param.9) | copy-start | bytes 884740
  42.2 40.1 %all-to-all-start = ((bf16[128,2,640]{2,1,0:T(2,128)(2,1)}), bf16[128,2,640]{2,1,0:T(2,128)(2,1)S(1)}, u32[]{:S(2)}, u32[]{:S(2)}) async-start(bf16[128,2,640]{2,1,0:T(2,128)(2,1)} %get-tuple-element.41), calls=%async_computation | async-start | bytes 655360 | tf_op jit(solution)/shard_map/all_to_all | solution.py:403
  62.5 17.2 %collective-permute-start.2 = (bf16[64,2304]{1,0:T(8,128)(2,1)S(1)}, bf16[64,2304]{1,0:T(8,128)(2,1)S(1)}, u32[]{:S(2)}, u32[]{:S(2)}) collective-permute-start(bf16[64,2304]{1,0:T(8,128)(2,1)S(1)} %bitcast.27), channel_id=1, source_target_pairs={{0,2},{1,3},{2,0},{3,1},{4,6},{5,7},{6,4},{7,5},{8,10},{9,11},{10,... | collective-permute-start | bytes 884744 | tf_op jit(solution)/shard_map/ppermute | solution.py:404
  65.3 6.4 %collective-permute-start.3 = (bf16[64,256]{1,0:T(8,128)(2,1)S(1)}, bf16[64,256]{1,0:T(8,128)(2,1)S(1)}, u32[]{:S(2)}, u32[]{:S(2)}) collective-permute-start(bf16[64,256]{1,0:T(8,128)(2,1)S(1)} %get-tuple-element.38), channel_id=1, source_target_pairs={{4,0},{0,4},{12,8},{8,12},{20,16},{16,20},{28,24},{24,28},{36,32},... | collective-permute-start | bytes 98312 | tf_op jit(solution)/shard_map/ppermute | solution.py:407
  67.8 3.9 %collective-permute-start.4 = (bf16[64,256]{1,0:T(8,128)(2,1)S(1)}, bf16[64,256]{1,0:T(8,128)(2,1)S(1)}, u32[]{:S(2)}, u32[]{:S(2)}) collective-permute-start(bf16[64,256]{1,0:T(8,128)(2,1)S(1)} %get-tuple-element.39), channel_id=1, source_target_pairs={{4,8},{8,4},{12,16},{16,12},{20,24},{24,20},{28,32},{32,28},{36,40... | collective-permute-start | bytes 98312 | tf_op jit(solution)/shard_map/ppermute | solution.py:406
  68.4 19.4 %collective-permute-start.1 = (bf16[64,2304]{1,0:T(8,128)(2,1)S(1)}, bf16[64,2304]{1,0:T(8,128)(2,1)S(1)}, u32[]{:S(2)}, u32[]{:S(2)}) collective-permute-start(bf16[64,2304]{1,0:T(8,128)(2,1)S(1)} %bitcast.28), channel_id=1, source_target_pairs={{0,1},{1,0},{2,3},{3,2},{4,5},{5,4},{6,7},{7,6},{8,9},{9,8},{10,11... | collective-permute-start | bytes 884744 | tf_op jit(solution)/shard_map/ppermute | solution.py:405
  79.7 8.2 %collective-permute-start.5 = (bf16[64,2304]{1,0:T(8,128)(2,1)S(1)}, bf16[64,2304]{1,0:T(8,128)(2,1)S(1)}, u32[]{:S(2)}, u32[]{:S(2)}) collective-permute-start(bf16[64,2304]{1,0:T(8,128)(2,1)S(1)} %collective-permute-done.2.across_ref), channel_id=1, source_target_pairs={{0,1},{1,0},{2,3},{3,2},{4,5},{5,4},{6,7},{7,6},{8,9},{9,8},{10,11... | collective-permute-start | bytes 884744 | tf_op jit(solution)/shard_map/ppermute | solution.py:409

commit v5 on v4

--- a/solution.py
+++ b/solution.py
@@ -405,8 +405,7 @@
     beside = lax.ppermute(turned, "cols", [(i, i ^ 1) for i in range(4)])
     two = lax.ppermute(two, "rows", far_pairs)
     one = lax.ppermute(one, "rows", near_pairs)
-    across, one, two = lax.optimization_barrier((across, one, two))
-    corner = lax.ppermute(across, "cols", [(i, i ^ 1) for i in range(4)])
+    corner = lax.ppermute(turned, "cols", [(i, i ^ 3) for i in range(4)])
     (share,) = call(
         functools.partial(share_kernel, 1.0 / math.sqrt(1024 * count)),
         [shape((32, 128), BF)],
@@ -417,7 +416,7 @@
         [pltpu.VMEM],
     )(part)
     share = lax.all_gather(share, "cols", axis=0)
-    share, one, two = lax.optimization_barrier((share, one, two))
+    share, one, two, across, beside, corner = lax.optimization_barrier((share, one, two, across, beside, corner))
     fine_out, grad_input, grad_weight = call(
         fine_kernel,
         [shape((256, 256), BF), shape((256, 256), BF), shape((18, 256), F32)],

time: 90 us -> 90 us (level)
  blocking collectives: 40.2 us -> 42.4 us
  waiting for transfers between devices: 8.01 us -> 6.67 us
    ppermute x1, waiting for transfers between devices: 8 us -> 0.01 us  [on_device(): across = lax.ppermute(turned, 'cols', [(i, i ^ 2) for i in range(4)])]
    all_to_all x1, waiting for transfers between devices: 0.01 us -> 6.66 us  [on_device(): part = lax.all_to_all(part, 'rows', 0, 0, tiled=True)]
    all_gather x1, blocking collectives: 5.06 us -> 7.23 us  [on_device(): share = lax.all_gather(share, 'cols', axis=0)]
    ppermute x1, starting transfers between devices: 3.19 us -> 1.98 us  [on_device(): beside = lax.ppermute(turned, 'cols', [(i, i ^ 1) for i in range(4)])]
where the time goes in v5:
time: 90 us; the launch traced here: 89.5 us
  blocking collectives  42.4 us (47%)
  starting transfers between devices  31.9 us (35%)
  Pallas kernels  7.73 us (9%)
  waiting for transfers between devices  6.67 us (7%)
    all_to_all x1, starting transfers between devices, on_device(): part = lax.all_to_all(part, 'rows', 0, 0, tiled=True)  20.3 us
    all_gather x1, blocking collectives, on_device(): near = lax.all_gather(jnp.concatenate([one, two], axis=0), 'cols', axis=0)  10.9 us
    all_gather x1, blocking collectives, on_device(): sec = lax.all_gather(sec, 'cols', axis=0)  9.43 us
    all_gather x1, blocking collectives, on_device(): late = lax.all_gather(late, 'cols', axis=0)  8.01 us
    all_gather x1, blocking collectives, on_device(): share = lax.all_gather(share, 'cols', axis=0)  7.23 us
    all_gather x1, blocking collectives, on_device(): lax.all_gather(one, 'rows', axis=0, tiled=True, axis_index_groups=pairs)  6.73 us
    all_to_all x1, waiting for transfers between devices, on_device(): part = lax.all_to_all(part, 'rows', 0, 0, tiled=True)  6.66 us
    ppermute x1, starting transfers between devices, on_device(): corner = lax.ppermute(turned, 'cols', [(i, i ^ 3) for i in range(4)])  3.14 us
  transfers between devices with their start and end apart: 7, of which 1 were waited for; matrix products, arithmetic and copies ran while one was open for 0% of the time, Pallas kernels for 1%

profile of v5, /device:TPU:1, one launch (start us, length us, event | category | flops | bytes accessed | tf_op | source)
XLA Modules:
  0.0 89.5 jit_solution(7069535843011776078)
XLA Ops:
  0.6 0.0 copy-start
  0.6 0.0 copy-start.3
  0.7 0.0 copy-start.4
  0.7 0.0 copy-start.5
  0.7 1.6 %pack.1 = (bf16[64,256]{1,0:T(8,128)(2,1)}, bf16[64,256]{1,0:T(8,128)(2,1)}) custom-call(bf16[256,256]{1,0:T(8,128)(2,1)} %bitcast.21, bf16[16,512]{1,0:T(8,128)(2,1)} %bitcast.31), custom_call_target="tpu_custom_call" | custom-call | flops 20971520000 | bytes 1048576 | tf_op jit(solution)/shard_map/pack/pallas_call | solution.py:347
  2.2 0.7 collective-permute-start
  2.9 6.7 %all_gather.27 = bf16[128,256]{1,0:T(8,128)(2,1)S(1)} all-gather(bf16[64,256]{1,0:T(8,128)(2,1)} %get-tuple-element.28), channel_id=1, replica_groups={{0,4},{8,12},{16,20},{24,28},{32,36},{40,44},{48,52},{56,60},{64,68},{7..., dimensions={0}, use_global_device_ids=true | all-gather | bytes 98304 | tf_op jit(solution)/shard_map/all_gather | solution.py:358
  9.6 0.0 collective-permute-done
  9.7 10.9 %all-gather = bf16[768,256]{1,0:T(8,128)(2,1)S(1)} all-gather(bf16[192,256]{1,0:T(8,128)(2,1)S(1)} %pad_maximum_fusion), channel_id=2, replica_groups=mesh['rows'=128,'cols'=4] {'cols'}, dimensions={0}, use_global_device_ids=true | all-gather | bytes 491520 | tf_op jit(solution)/shard_map/all_gather | solution.py:359
  20.6 0.0 copy-done
  20.6 0.0 copy-done.3
  20.6 0.0 copy-done.4
  20.6 0.0 copy-done.5
  20.6 0.0 copy-start.1
  20.6 0.0 copy-start.2
  20.7 0.9 first.1
  21.5 9.4 %all-gather.1 = bf16[3584,128]{1,0:T(8,128)(2,1)S(1)} all-gather(bf16[896,128]{1,0:T(8,128)(2,1)S(1)} %get-tuple-element.30), channel_id=3, replica_groups=mesh['rows'=128,'cols'=4] {'cols'}, dimensions={0}, use_global_device_ids=true | all-gather | bytes 1146880 | tf_op jit(solution)/shard_map/all_gather | solution.py:376
  31.0 0.0 copy-done.1
  31.0 0.0 copy-done.2
  31.0 0.6 second.1
  31.6 8.0 %all-gather.2 = bf16[2560,128]{1,0:T(8,128)(2,1)S(1)} all-gather(bf16[640,128]{1,0:T(8,128)(2,1)S(1)} %second.1), channel_id=4, replica_groups=mesh['rows'=128,'cols'=4] {'cols'}, dimensions={0}, use_global_device_ids=true | all-gather | bytes 819200 | tf_op jit(solution)/shard_map/all_gather | solution.py:386
  39.6 0.0 copy-start.6
  39.6 2.6 %grad.1 = (bf16[128,2,640]{2,1,0:T(2,128)(2,1)}, bf16[8,64,256]{2,1,0:T(8,128)(2,1)S(1)}, bf16[64,256]{1,0:T(8,128)(2,1)S(1)}, bf16[64,256]{1,0:T(8,128)(2,1)S(1)}, bf16[16,512]{1,0:T(8,128)(2,1)}) custom-call(bf16[4,192,256]{2,1,0:T(8,128)(2,1)S(1)} %bitcast.17, bf16[4,896,128]{2,1,0:T(8,128)(2,1)S(1)} %bitcast.14, bf16[4,640,128]{2,1,0:T(8,128)(2,1)S(1)} %bitcast.19), custom_call_target="tpu_custom_call" | custom-call | flops 1048576000 | bytes 1048576 | tf_op jit(solution)/shard_map/grad/pallas_call | solution.py:387
  42.2 20.3 %all-to-all-start = ((bf16[128,2,640]{2,1,0:T(2,128)(2,1)}), bf16[128,2,640]{2,1,0:T(2,128)(2,1)S(1)}, u32[]{:S(2)}, u32[]{:S(2)}) async-start(bf16[128,2,640]{2,1,0:T(2,128)(2,1)} %get-tuple-element.38), calls=%async_computation | async-start | bytes 655360 | tf_op jit(solution)/shard_map/all_to_all | solution.py:403
  62.5 0.0 copy-done.6
  62.5 3.1 %collective-permute-start.5 = (bf16[64,2304]{1,0:T(8,128)(2,1)S(1)}, bf16[64,2304]{1,0:T(8,128)(2,1)S(1)}, u32[]{:S(2)}, u32[]{:S(2)}) collective-permute-start(bf16[64,2304]{1,0:T(8,128)(2,1)S(1)} %bitcast.27), channel_id=1, source_target_pairs={{0,3},{1,2},{2,1},{3,0},{4,7},{5,6},{6,5},{7,4},{8,11},{9,10},{10,... | collective-permute-start | bytes 884744 | tf_op jit(solution)/shard_map/ppermute | solution.py:408
  65.6 2.0 %collective-permute-start.4 = (bf16[64,2304]{1,0:T(8,128)(2,1)S(1)}, bf16[64,2304]{1,0:T(8,128)(2,1)S(1)}, u32[]{:S(2)}, u32[]{:S(2)}) collective-permute-start(bf16[64,2304]{1,0:T(8,128)(2,1)S(1)} %bitcast.28), channel_id=1, source_target_pairs={{0,1},{1,0},{2,3},{3,2},{4,5},{5,4},{6,7},{7,6},{8,9},{9,8},{10,11... | collective-permute-start | bytes 884744 | tf_op jit(solution)/shard_map/ppermute | solution.py:405
  67.6 2.5 %collective-permute-start.3 = (bf16[64,2304]{1,0:T(8,128)(2,1)S(1)}, bf16[64,2304]{1,0:T(8,128)(2,1)S(1)}, u32[]{:S(2)}, u32[]{:S(2)}) collective-permute-start(bf16[64,2304]{1,0:T(8,128)(2,1)S(1)} %bitcast.29), channel_id=1, source_target_pairs={{0,2},{1,3},{2,0},{3,1},{4,6},{5,7},{6,4},{7,5},{8,10},{9,11},{10,... | collective-permute-start | bytes 884744 | tf_op jit(solution)/shard_map/ppermute | solution.py:404
  70.1 2.7 %collective-permute-start.1 = (bf16[64,256]{1,0:T(8,128)(2,1)S(1)}, bf16[64,256]{1,0:T(8,128)(2,1)S(1)}, u32[]{:S(2)}, u32[]{:S(2)}) collective-permute-start(bf16[64,256]{1,0:T(8,128)(2,1)S(1)} %get-tuple-element.39), channel_id=1, source_target_pairs={{4,0},{0,4},{12,8},{8,12},{20,16},{16,20},{28,24},{24,28},{36,32},... | collective-permute-start | bytes 98312 | tf_op jit(solution)/shard_map/ppermute | solution.py:407
  72.8 0.7 collective-permute-start.2
  73.5 6.7 %all-to-all-done.part_ref = bf16[128,2,640]{2,1,0:T(2,128)(2,1)S(1)} async-done(((bf16[128,2,640]{2,1,0:T(2,128)(2,1)}), bf16[128,2,640]{2,1,0:T(2,128)(2,1)S(1)}, u32[]{:S(2)}, u32[]{:S(2)}) %all-to-all-start) | async-done | bytes 327712 | tf_op jit(solution)/shard_map/all_to_all | solution.py:403
  80.1 0.5 share.1
  80.6 7.2 %all-gather.3 = bf16[128,128]{1,0:T(8,128)(2,1)S(1)} all-gather(bf16[32,128]{1,0:T(8,128)(2,1)S(1)} %share.1), channel_id=5, replica_groups=mesh['rows'=128,'cols'=4] {'cols'}, dimensions={0}, use_global_device_ids=true | all-gather | bytes 40960 | tf_op jit(solution)/shard_map/all_gather | solution.py:418
  87.9 0.0 collective-permute-done.1.one_ref
  87.9 0.0 collective-permute-done.2.two_ref
  87.9 0.0 collective-permute-done.5.corner_ref
  87.9 0.0 collective-permute-done.4.beside_ref
  87.9 0.0 collective-permute-done.3.across_ref
  87.9 1.6 %fine.1 = (bf16[256,256]{1,0:T(8,128)(2,1)}, bf16[256,256]{1,0:T(8,128)(2,1)}, f32[18,256]{1,0:T(8,128)}) custom-call(bf16[4,192,256]{2,1,0:T(8,128)(2,1)S(1)} %bitcast.18, bf16[4,896,128]{2,1,0:T(8,128)(2,1)S(1)} %bitcast.15, bf16[64,2304]{1,0:T(8,128)(2,1)S(1)} %bitcast.30, bf16[64,2304]{1,0:T(8,128)(2,1)S(1)} %collective-permute-done.4.beside_ref, ...), custom_call_target="tpu_custom_call" | custom-call | flops 1048576000 | bytes 1048576 | tf_op jit(solution)/shard_map/fine/pallas_call | solution.py:420
  (1 shorter events, 0.0 us)
Async XLA Ops:
  0.6 20.0 %copy-start = (bf16[4608,128]{1,0:T(8,128)(2,1)S(1)}, bf16[4608,128]{1,0:T(8,128)(2,1)}, u32[]{:S(2)}) copy-start(bf16[4608,128]{1,0:T(8,128)(2,1)} %teacher_ref.3) | copy-start | bytes 3538948
  0.6 20.0 %copy-start.3 = (bf16[8,32,256]{2,1,0:T(8,128)(2,1)S(1)}, bf16[8,32,256]{2,1,0:T(8,128)(2,1)}, u32[]{:S(2)}) copy-start(bf16[8,32,256]{2,1,0:T(8,128)(2,1)} %param.15) | copy-start | bytes 393220
  0.7 20.0 %copy-start.4 = (bf16[512,64]{0,1:T(8,128)(2,1)S(1)}, bf16[512,64]{0,1:T(8,128)(2,1)}, u32[]{:S(2)}) copy-start(bf16[512,64]{0,1:T(8,128)(2,1)} %param.10) | copy-start | bytes 196612
  0.7 20.0 %copy-start.5 = (s32[3]{0:T(128)S(1)}, s32[3]{0:T(128)}, u32[]{:S(2)}) copy-start(s32[3]{0:T(128)} %param.14) | copy-start | bytes 40
  2.2 7.4 %collective-permute-start = (bf16[64,256]{1,0:T(8,128)(2,1)}, bf16[64,256]{1,0:T(8,128)(2,1)S(1)}, u32[]{:S(2)}, u32[]{:S(2)}) collective-permute-start(bf16[64,256]{1,0:T(8,128)(2,1)} %get-tuple-element.29), channel_id=1, source_target_pairs={{4,8},{8,4},{12,16},{16,12},{20,24},{24,20},{28,32},{32,28},{36,40... | collective-permute-start | bytes 98312 | tf_op jit(solution)/shard_map/ppermute | solution.py:356
  20.6 10.3 %copy-start.1 = (bf16[4608,128]{1,0:T(8,128)(2,1)S(1)}, bf16[4608,128]{1,0:T(8,128)(2,1)}, u32[]{:S(2)}) copy-start(bf16[4608,128]{1,0:T(8,128)(2,1)} %student_ref.1) | copy-start | bytes 3538948
  20.6 10.3 %copy-start.2 = (bf16[8,32,256]{2,1,0:T(8,128)(2,1)S(1)}, bf16[8,32,256]{2,1,0:T(8,128)(2,1)}, u32[]{:S(2)}) copy-start(bf16[8,32,256]{2,1,0:T(8,128)(2,1)} %param.8) | copy-start | bytes 393220
  39.6 22.9 %copy-start.6 = (bf16[2304,64]{0,1:T(8,128)(2,1)S(1)}, bf16[2304,64]{0,1:T(8,128)(2,1)}, u32[]{:S(2)}) copy-start(bf16[2304,64]{0,1:T(8,128)(2,1)} %param.9) | copy-start | bytes 884740
  42.2 37.9 %all-to-all-start = ((bf16[128,2,640]{2,1,0:T(2,128)(2,1)}), bf16[128,2,640]{2,1,0:T(2,128)(2,1)S(1)}, u32[]{:S(2)}, u32[]{:S(2)}) async-start(bf16[128,2,640]{2,1,0:T(2,128)(2,1)} %get-tuple-element.38), calls=%async_computation | async-start | bytes 655360 | tf_op jit(solution)/shard_map/all_to_all | solution.py:403
  62.5 25.4 %collective-permute-start.5 = (bf16[64,2304]{1,0:T(8,128)(2,1)S(1)}, bf16[64,2304]{1,0:T(8,128)(2,1)S(1)}, u32[]{:S(2)}, u32[]{:S(2)}) collective-permute-start(bf16[64,2304]{1,0:T(8,128)(2,1)S(1)} %bitcast.27), channel_id=1, source_target_pairs={{0,3},{1,2},{2,1},{3,0},{4,7},{5,6},{6,5},{7,4},{8,11},{9,10},{10,... | collective-permute-start | bytes 884744 | tf_op jit(solution)/shard_map/ppermute | solution.py:408
  65.6 22.3 %collective-permute-start.4 = (bf16[64,2304]{1,0:T(8,128)(2,1)S(1)}, bf16[64,2304]{1,0:T(8,128)(2,1)S(1)}, u32[]{:S(2)}, u32[]{:S(2)}) collective-permute-start(bf16[64,2304]{1,0:T(8,128)(2,1)S(1)} %bitcast.28), channel_id=1, source_target_pairs={{0,1},{1,0},{2,3},{3,2},{4,5},{5,4},{6,7},{7,6},{8,9},{9,8},{10,11... | collective-permute-start | bytes 884744 | tf_op jit(solution)/shard_map/ppermute | solution.py:405
  67.6 20.3 %collective-permute-start.3 = (bf16[64,2304]{1,0:T(8,128)(2,1)S(1)}, bf16[64,2304]{1,0:T(8,128)(2,1)S(1)}, u32[]{:S(2)}, u32[]{:S(2)}) collective-permute-start(bf16[64,2304]{1,0:T(8,128)(2,1)S(1)} %bitcast.29), channel_id=1, source_target_pairs={{0,2},{1,3},{2,0},{3,1},{4,6},{5,7},{6,4},{7,5},{8,10},{9,11},{10,... | collective-permute-start | bytes 884744 | tf_op jit(solution)/shard_map/ppermute | solution.py:404
  70.1 17.8 %collective-permute-start.1 = (bf16[64,256]{1,0:T(8,128)(2,1)S(1)}, bf16[64,256]{1,0:T(8,128)(2,1)S(1)}, u32[]{:S(2)}, u32[]{:S(2)}) collective-permute-start(bf16[64,256]{1,0:T(8,128)(2,1)S(1)} %get-tuple-element.39), channel_id=1, source_target_pairs={{4,0},{0,4},{12,8},{8,12},{20,16},{16,20},{28,24},{24,28},{36,32},... | collective-permute-start | bytes 98312 | tf_op jit(solution)/shard_map/ppermute | solution.py:407
  72.8 15.1 %collective-permute-start.2 = (bf16[64,256]{1,0:T(8,128)(2,1)S(1)}, bf16[64,256]{1,0:T(8,128)(2,1)S(1)}, u32[]{:S(2)}, u32[]{:S(2)}) collective-permute-start(bf16[64,256]{1,0:T(8,128)(2,1)S(1)} %get-tuple-element.40), channel_id=1, source_target_pairs={{4,8},{8,4},{12,16},{16,12},{20,24},{24,20},{28,32},{32,28},{36,40... | collective-permute-start | bytes 98312 | tf_op jit(solution)/shard_map/ppermute | solution.py:406
